TPU v7x, 256 devices: a whole 4x4x8 slice. The times are simulated.
256 devices in a mesh: gy: 32 (over z_hi, y, x), gz: 8 (over z_lo, core).
Axes of the slice: x: 4, y: 4, z: 8 (z_hi: 2, z_lo: 4; z = z_hi * 4 + z_lo), core: 2. Of those that a mesh axis runs over, the one named last changes fastest.
Arguments:
- kspace: float32 [2, 4, 256, 32, 256], P(None, None, 'gy', 'gz'), may hold values from -6 to 6
- cotangent: float32 [2, 4, 256, 32, 256], P(None, None, 'gy', 'gz'), may hold values from -6 to 6
- weight_in: bfloat16 [16, 8, 3, 3, 3], replicated, may hold values from -0.4375 to 0.4375
- weight_out: bfloat16 [8, 16, 3, 3, 3], replicated, may hold values from -0.3125 to 0.3125
- consistency_weight: float32 [1], replicated, may hold values from 0.2 to 1
- sampling_mask: int32 [256, 32], P('gy', 'gz'), may hold values 0 or 1
Outputs:
- grad_kspace: float32 [2, 4, 256, 32, 256], P(None, None, 'gy', 'gz')
- grad_weight_in: float32 [16, 8, 3, 3, 3], replicated
- grad_weight_out: float32 [8, 16, 3, 3, 3], replicated
Inputs may be any that keep to these rules, and one draw needn't show every extreme that they name: `sampling_mask`: 1 marks a sampled phase-encode line.
All inputs are finite; a program needn't handle non-finite values. No bound on the sum of `sampling_mask` on one device may be relied on, other than what follows from the above.
Results may differ from a plain program's by a relative error of at most 0.0059.
Values may be sent and summed in bfloat16 or wider, within the bound.
A program may use at most 128 MiB of HBM per device.

v0:
```python
import math

import jax
import jax.numpy as jnp
from jax import lax
from jax.sharding import PartitionSpec as P


def as_sent(shard):
    return jax.tree.map(lambda a: a.astype(jnp.bfloat16) if a.dtype == jnp.float32 else a, shard)


def extended(shard, sides, width):
    for axis, dim in sides:
        count, length = (lax.axis_size(axis), shard.shape[dim])
        up = [(i, (i + 1) % count) for i in range(count - 1)]
        down = [(j, i) for i, j in up]
        last = lax.slice_in_dim(shard, length - width, length, axis=dim)
        first = lax.slice_in_dim(shard, 0, width, axis=dim)
        before = lax.ppermute(last, axis, up)
        after = lax.ppermute(first, axis, down)
        shard = jnp.concatenate([before, shard, after], axis=dim)
    return shard


def dft_table(length, direction):
    indices = lax.iota(jnp.int32, length)
    products = indices[:, None] * indices[None, :] % length
    phases = products.astype(jnp.float32) * (2.0 * math.pi / length)
    cosine = jnp.cos(phases) / math.sqrt(length)
    sine_part = direction * jnp.sin(phases) / math.sqrt(length)
    return jnp.stack([jnp.stack([cosine, -sine_part]), jnp.stack([sine_part, cosine])])


def spectral(spectrum, direction):
    field_parts = spectrum.shape[1]
    cells_y = spectrum.shape[2]
    cells_z = spectrum.shape[3]
    readout = spectrum.shape[4]
    length_y = cells_y * lax.axis_size("gy")
    length_z = cells_z * lax.axis_size("gz")
    table_y = dft_table(length_y, direction)
    table_z = dft_table(length_z, direction)
    flattened = spectrum.reshape(2, field_parts, cells_y, cells_z * readout)
    transformed_y = jnp.einsum(
        "pqvy,qcym->pcvm",
        table_y,
        lax.all_to_all(flattened, "gy", split_axis=3, concat_axis=2, tiled=True),
        precision=lax.Precision.HIGHEST,
    )
    turned_field = lax.all_to_all(
        lax.all_to_all(transformed_y, "gy", split_axis=2, concat_axis=3, tiled=True),
        "gz",
        split_axis=2,
        concat_axis=3,
        tiled=True,
    )
    shaped = turned_field.reshape(
        turned_field.shape[0], turned_field.shape[1], turned_field.shape[2], length_z, readout
    )
    turned = jnp.einsum("pqwz,qcyzx->pcywx", table_z, shaped, precision=lax.Precision.HIGHEST)
    transformed_z = turned.reshape(turned_field.shape)
    result = lax.all_to_all(
        as_sent(transformed_z), "gz", split_axis=3, concat_axis=2, tiled=True
    ).astype(transformed_z.dtype)
    return result.reshape(spectrum.shape)


def with_rims(volume):
    return extended(volume, (("gy", 2), ("gz", 3)), 1)


def convolve(padded, kernel):
    return lax.conv_general_dilated(
        padded,
        kernel,
        (1, 1, 1),
        ((0, 0), (0, 0), (1, 1)),
        dimension_numbers=("NCDHW", "OIDHW", "NCDHW"),
        preferred_element_type=jnp.float32,
    )


def kernel_gradient(padded, cotangent_part):
    summed = lax.conv_general_dilated(
        padded,
        cotangent_part,
        (1, 1, 1),
        ((0, 0), (0, 0), (1, 1)),
        dimension_numbers=("CNDHW", "IODHW", "NCDHW"),
        preferred_element_type=jnp.float32,
    )
    return summed.transpose(1, 0, 2, 3, 4)


def flipped(kernel):
    return jnp.flip(kernel, (2, 3, 4)).transpose(1, 0, 2, 3, 4)


def local(kspace, cotangent, weight_in, weight_out, consistency_weight, sampling_mask):
    coil_count = kspace.shape[1]
    channels = 2 * coil_count
    cells_y = kspace.shape[2]
    cells_z = kspace.shape[3]
    readout = kspace.shape[4]
    voxels = readout * cells_y * cells_z * lax.axis_size("gy") * lax.axis_size("gz")
    image_field = spectral(kspace, 1.0)
    back_field = spectral(cotangent, 1.0)
    image_in = image_field.astype(jnp.bfloat16).reshape(1, channels, cells_y, cells_z, readout)
    back_out = (-back_field).astype(jnp.bfloat16).reshape(1, channels, cells_y, cells_z, readout)
    image_padded = with_rims(image_in)
    back_padded = with_rims(back_out)
    hidden = convolve(image_padded, weight_in)
    active = jax.nn.silu(hidden).astype(jnp.bfloat16)
    active_padded = with_rims(active)
    local_out = kernel_gradient(active_padded, back_out)
    back_active = convolve(back_padded, flipped(weight_out))
    gate = jax.nn.sigmoid(hidden)
    back_hidden = (back_active * gate * (1.0 + hidden * (1.0 - gate))).astype(jnp.bfloat16)
    local_in = kernel_gradient(image_padded, back_hidden)
    hidden_padded = with_rims(back_hidden)
    back_image = convolve(hidden_padded, flipped(weight_in))
    spectrum = spectral(back_image.reshape(2, coil_count, cells_y, cells_z, readout), -1.0)
    summed_in, summed_out = lax.psum((local_in, local_out), ("gy", "gz"))
    scale = 1.0 / math.sqrt(voxels)
    mask_field = sampling_mask.astype(jnp.float32)[None, None, :, :, None]
    grad_kspace = cotangent - consistency_weight[0] * mask_field * cotangent + spectrum
    return (grad_kspace, summed_in * scale, summed_out * scale)


def solution(mesh):
    placed = (
        P(None, None, "gy", "gz", None),
        P(None, None, "gy", "gz", None),
        P(),
        P(),
        P(),
        P("gy", "gz"),
    )
    return jax.shard_map(
        local,
        mesh=mesh,
        in_specs=placed,
        out_specs=(P(None, None, "gy", "gz", None), P(), P()),
        check_vma=False,
    )
```

profile of v0, /device:TPU:1, one launch (start us, length us, event | category | flops | bytes accessed | tf_op | source)
XLA Modules:
  0.0 722.7 jit_solution(2760864033944492216)
XLA Ops:
  0.7 4.5 copy.348
  5.2 6.9 reshape.431
  12.1 14.5 %all-to-all-start.4 = ((f32[32,1,2048]{2,1,0:T(1,128)}), f32[32,1,2048]{2,1,0:T(1,128)S(1)}, u32[]{:S(2)}, u32[]{:S(2)}) async-start(f32[32,1,2048]{2,1,0:T(1,128)} %reshape.431), calls=%async_computation.4 | async-start | bytes 524288 | tf_op jit(solution)/shard_map/all_to_all | solution.py:48
  29.7 6.9 reshape.437
  38.5 11.0 %all-to-all-start = ((f32[32,1,2048]{2,1,0:T(1,128)}), f32[32,1,2048]{2,1,0:T(1,128)S(1)}, u32[]{:S(2)}, u32[]{:S(2)}) async-start(f32[32,1,2048]{2,1,0:T(1,128)} %reshape.437), calls=%async_computation | async-start | bytes 524288 | tf_op jit(solution)/shard_map/all_to_all | solution.py:48
  54.6 6.3 reshape.432
  68.4 12.0 %all-to-all-start.5 = ((f32[32,1,2048]{2,1,0:T(1,128)}), f32[32,1,2048]{2,1,0:T(1,128)S(1)}, u32[]{:S(2)}, u32[]{:S(2)}) async-start(f32[32,1,2048]{2,1,0:T(1,128)} %reshape.433), calls=%async_computation.5 | async-start | bytes 524288 | tf_op jit(solution)/shard_map/all_to_all | solution.py:52
  81.7 6.3 reshape.438
  95.5 11.8 %all-to-all-start.1 = ((f32[32,1,2048]{2,1,0:T(1,128)}), f32[32,1,2048]{2,1,0:T(1,128)S(1)}, u32[]{:S(2)}, u32[]{:S(2)}) async-start(f32[32,1,2048]{2,1,0:T(1,128)} %reshape.439), calls=%async_computation.1 | async-start | bytes 524288 | tf_op jit(solution)/shard_map/all_to_all | solution.py:52
  110.7 8.5 %all-to-all-done.1 = f32[32,1,2048]{2,1,0:T(1,128)S(1)} async-done(((f32[32,1,2048]{2,1,0:T(1,128)}), f32[32,1,2048]{2,1,0:T(1,128)S(1)}, u32[]{:S(2)}, u32[]{:S(2)}) %all-to-all-start.1) | async-done | bytes 262176 | tf_op jit(solution)/shard_map/all_to_all | solution.py:52
  119.2 7.4 %all-to-all-start.6 = ((f32[2,4,8,1024]{3,1,0,2:T(4,128)}), f32[2,4,8,1024]{3,1,0,2:T(4,128)S(1)}, u32[]{:S(2)}, u32[]{:S(2)}) async-start(f32[2,4,8,1024]{3,1,0,2:T(4,128)} %reshape.424), calls=%async_computation.6 | async-start | bytes 524288 | tf_op jit(solution)/shard_map/all_to_all | solution.py:51
  130.3 5.1 all-to-all-done.6
  135.4 4.8 all-to-all-start.2
  141.7 5.0 copy.421
  146.6 9.3 %reshape.435 = bf16[8,2,4096]{2,1,0:T(2,128)(2,1)} reshape(bf16[8192,1,2,4]{3,2,1,0:T(2,128)(2,1)} %bitcast.299) | data formatting | bytes 262144
  156.0 5.1 all-to-all-start.7
  162.4 5.0 copy.415
  167.4 9.3 %reshape.441 = bf16[8,2,4096]{2,1,0:T(2,128)(2,1)} reshape(bf16[8192,1,2,4]{3,2,1,0:T(2,128)(2,1)} %bitcast.300) | data formatting | bytes 262144
  176.7 5.1 all-to-all-start.3
  182.5 10.0 %reshape.436 = bf16[8192,1,2,4]{3,2,1,0:T(2,128)(2,1)} reshape(bf16[8,2,4096]{2,1,0:T(2,128)(2,1)S(1)} %all-to-all-done.7) | data formatting | bytes 262144
  192.6 8.6 %copy.358 = bf16[2,4,1,8192]{3,1,0,2:T(4,128)(2,1)S(1)} copy(bf16[2,4,1,8192]{1,0,2,3:T(2,128)(2,1)} %bitcast.301) | data formatting | bytes 262144 | tf_op jit(solution)/shard_map/all_to_all | solution.py:63
  203.3 10.1 %reshape.442 = bf16[8192,1,2,4]{3,2,1,0:T(2,128)(2,1)} reshape(bf16[8,2,4096]{2,1,0:T(2,128)(2,1)S(1)} %all-to-all-done.3) | data formatting | bytes 262144
  213.4 8.6 %copy.344 = bf16[2,4,1,8192]{3,1,2,0:T(4,128)(2,1)S(1)} copy(bf16[2,4,1,8192]{1,0,2,3:T(2,128)(2,1)} %bitcast.302) | data formatting | bytes 262144 | tf_op jit(solution)/shard_map/all_to_all | solution.py:63
  222.2 7.4 %copy.396 = bf16[1,8,8,4,256]{1,0,4,3,2:T(2,128)(2,1)} copy(bf16[1,8,8,4,256]{4,3,2,1,0:T(4,128)(2,1)S(1)} %convert_element_type.199) | data formatting | bytes 262144 | tf_op jit(solution)/shard_map/convert_element_type | solution.py:110
  254.5 4.8 copy.361
  263.3 4.6 copy.347
  269.0 9.1 %multiply_convert_fusion.1 = (bf16[8,4,8,33,16]{4,2,3,1,0:T(8,128)(2,1)}, f32[8,4,8,33,16]{4,2,3,1,0:T(8,128)S(1)}) fusion(pred[8,33]{0,1:T(8,128)(4,1)S(1)} %copy-done.15, bf16[16,8,3,3,3]{0,1,4,3,2:T(8,128)(2,1)S(1)} %copy-done, bf16[8,10,6,1,7,2]{0,4,5,2,1,3:T(8,128)(2,1)S(1)} %copy-done.8, bf16[8,10,6,1,8,33]{0,4,5,2,1,3:T(8,128)(2,1)} %copy.361), kind=kOutput, calls=%fused_computation.16 | convolution fusion | flops 60009984 | bytes 1085064 | tf_op jit(solution)/shard_map/conv_general_dilated | solution.py:74
  278.2 9.5 %multiply_convert_fusion = bf16[8,4,8,33,16]{4,2,3,1,0:T(8,128)(2,1)} fusion(f32[8,4,8,33,16]{4,2,3,1,0:T(8,128)S(1)} %get-tuple-element.36, bf16[8,16,3,3,3]{1,0,4,3,2:T(8,128)(2,1)S(1)} %copy-done.14, bf16[8,10,6,1,7,2]{0,4,5,2,1,3:T(8,128)(2,1)S(1)} %slice.86, bf16[8,10,6,1,8,33]{0,4,5,2,1,3:T(8,128)(2,1)S(1)} %copy-done.2, pred[8,33]{0,1:T(8,128)(4,1)S(1)} %copy-done.15), kind=kOutput, calls=%fused_computation.15 | convolution fusion | flops 60685824 | bytes 1085064 | tf_op jit(solution)/shard_map/conv_general_dilated | solution.py:74
  296.9 5.2 collective-permute-start.12
  312.5 4.8 copy.442
  340.1 4.7 copy.368
  345.9 9.1 %broadcast_select_fusion = f32[8,4,8,33,8]{4,2,3,1,0:T(8,128)} fusion(pred[8,33]{0,1:T(8,128)(4,1)S(1)} %copy-done.15, bf16[16,8,3,3,3]{0,1,4,3,2:T(8,128)(2,1)S(1)} %copy-done, bf16[16,10,6,1,7,2]{0,4,5,2,1,3:T(8,128)(2,1)S(1)} %slice.97, bf16[16,10,6,1,8,33]{0,4,5,2,1,3:T(8,128)(2,1)} %copy.368), kind=kOutput, calls=%fused_computation.41 | convolution fusion | flops 60072960 | bytes 811272 | tf_op jit(solution)/shard_map/conv_general_dilated | solution.py:74
  361.5 6.9 reshape.443
  368.4 37.0 %all-to-all-start.8 = ((f32[32,1,2048]{2,1,0:T(1,128)}), f32[32,1,2048]{2,1,0:T(1,128)S(1)}, u32[]{:S(2)}, u32[]{:S(2)}) async-start(f32[32,1,2048]{2,1,0:T(1,128)} %reshape.443), calls=%async_computation.8 | async-start | bytes 524288 | tf_op jit(solution)/shard_map/all_to_all | solution.py:48
  414.7 4.5 copy.388
  427.8 6.4 reshape.444
  437.8 5.4 convolution_bitcast_fusion.5
  446.6 12.3 %all-to-all-start.9 = ((f32[32,1,2048]{2,1,0:T(1,128)}), f32[32,1,2048]{2,1,0:T(1,128)S(1)}, u32[]{:S(2)}, u32[]{:S(2)}) async-start(f32[32,1,2048]{2,1,0:T(1,128)} %reshape.445), calls=%async_computation.9 | async-start | bytes 524288 | tf_op jit(solution)/shard_map/all_to_all | solution.py:52
  458.9 22.9 %fusion.52 = f32[16,8,3,3,3]{0,1,4,3,2:T(8,128)} fusion(bf16[8,4,8,33,16]{4,2,3,1,0:T(8,128)(2,1)S(1)} %copy-done.5, pred[8,33]{0,1:T(8,128)(4,1)S(1)} %copy-done.15, bf16[8,10,6,8,33,1]{3,0,5,4,2,1:T(8,128)(2,1)} %fusion.33, bf16[8,10,6,8,33,1]{3,0,5,4,2,1:T(8,128)(2,1)} %copy.388, bf16[8,10,6,8,33,1]{3,0,5,4,2,1:T(8,128)(2,1)} %fusion.35), kind=kOutput, calls=%fused_computation.59 | convolution fusion | flops 59288064 | bytes 1044744 | tf_op jit(solution)/shard_map/transpose | solution.py:93
  482.8 12.0 %copy.395 = bf16[1,16,10,6,256]{1,0,4,3,2:T(2,128)(2,1)} copy(bf16[1,16,10,6,256]{4,1,3,2,0:T(8,128)(2,1)S(1)} %pad_maximum_fusion.7) | data formatting | bytes 983040 | tf_op jit(solution)/shard_map/concatenate | solution.py:22
  498.6 5.5 all-to-all-start.10
  504.1 90.1 %fusion.123 = f32[8,16,3,3,3]{1,0,4,3,2:T(8,128)S(1)} fusion(bf16[1,16,10,6,256]{1,0,4,3,2:T(2,128)(2,1)} %copy.395, bf16[1,8,8,4,256]{1,0,4,3,2:T(2,128)(2,1)} %copy.396), kind=kOutput, calls=%fused_computation.182 | convolution fusion | flops 56475648 | bytes 636416 | tf_op jit(solution)/shard_map/transpose | solution.py:93
  594.2 82.3 %all-reduce = (f32[16,8,3,3,3]{0,1,4,3,2:T(8,128)S(1)}, f32[8,16,3,3,3]{1,0,4,3,2:T(8,128)S(1)}) all-reduce(f32[16,8,3,3,3]{0,1,4,3,2:T(8,128)S(1)} %copy-done.11, f32[8,16,3,3,3]{1,0,4,3,2:T(8,128)S(1)} %fusion.123), channel_id=1, replica_groups=mesh['gy'=32,'gz'=8] {'gy','gz'}, use_global_device_ids=true, to_apply=%region_0.1 | all-reduce | flops 6912 | bytes 55296 | tf_op jit(solution)/shard_map/psum | solution.py:124
  677.9 5.0 copy.428
  682.8 9.3 %reshape.447 = bf16[8,2,4096]{2,1,0:T(2,128)(2,1)} reshape(bf16[8192,1,2,4]{3,2,1,0:T(2,128)(2,1)} %bitcast.304) | data formatting | bytes 262144
  696.8 5.2 all-to-all-done.11
  701.9 10.0 %reshape.448 = bf16[8192,1,2,4]{3,2,1,0:T(2,128)(2,1)} reshape(bf16[8,2,4096]{2,1,0:T(2,128)(2,1)S(1)} %all-to-all-done.11) | data formatting | bytes 262144
  712.0 9.6 %copy.381 = f32[2,4,8,4,256]{4,3,2,1,0:T(4,128)S(1)} copy(bf16[2,4,8,4,256]{1,0,4,3,2:T(2,128)(2,1)} %bitcast.305) | data formatting | bytes 393216 | tf_op jit(solution)/shard_map/convert_element_type | solution.py:65
  (188 shorter events, 154.2 us)
Async XLA Ops:
  0.6 268.4 %copy-start = (bf16[16,8,3,3,3]{0,1,4,3,2:T(8,128)(2,1)S(1)}, bf16[16,8,3,3,3]{0,1,4,3,2:T(8,128)(2,1)}, u32[]{:S(2)}) copy-start(bf16[16,8,3,3,3]{0,1,4,3,2:T(8,128)(2,1)} %param.8) | copy-start | bytes 20740
  0.6 25.9 %copy-start.6 = (f32[2,4,8,4,256]{4,3,2,1,0:T(4,128)S(1)}, f32[2,4,8,4,256]{4,3,2,1,0:T(4,128)}, u32[]{:S(2)}) copy-start(f32[2,4,8,4,256]{4,3,2,1,0:T(4,128)} %param.7) | copy-start | bytes 786436
  12.1 26.5 %all-to-all-start.4 = ((f32[32,1,2048]{2,1,0:T(1,128)}), f32[32,1,2048]{2,1,0:T(1,128)S(1)}, u32[]{:S(2)}, u32[]{:S(2)}) async-start(f32[32,1,2048]{2,1,0:T(1,128)} %reshape.431), calls=%async_computation.4 | async-start | bytes 524288 | tf_op jit(solution)/shard_map/all_to_all | solution.py:48
  38.5 29.9 %all-to-all-start = ((f32[32,1,2048]{2,1,0:T(1,128)}), f32[32,1,2048]{2,1,0:T(1,128)S(1)}, u32[]{:S(2)}, u32[]{:S(2)}) async-start(f32[32,1,2048]{2,1,0:T(1,128)} %reshape.437), calls=%async_computation | async-start | bytes 524288 | tf_op jit(solution)/shard_map/all_to_all | solution.py:48
  68.4 27.1 %all-to-all-start.5 = ((f32[32,1,2048]{2,1,0:T(1,128)}), f32[32,1,2048]{2,1,0:T(1,128)S(1)}, u32[]{:S(2)}, u32[]{:S(2)}) async-start(f32[32,1,2048]{2,1,0:T(1,128)} %reshape.433), calls=%async_computation.5 | async-start | bytes 524288 | tf_op jit(solution)/shard_map/all_to_all | solution.py:52
  95.5 23.8 %all-to-all-start.1 = ((f32[32,1,2048]{2,1,0:T(1,128)}), f32[32,1,2048]{2,1,0:T(1,128)S(1)}, u32[]{:S(2)}, u32[]{:S(2)}) async-start(f32[32,1,2048]{2,1,0:T(1,128)} %reshape.439), calls=%async_computation.1 | async-start | bytes 524288 | tf_op jit(solution)/shard_map/all_to_all | solution.py:52
  119.2 16.2 %all-to-all-start.6 = ((f32[2,4,8,1024]{3,1,0,2:T(4,128)}), f32[2,4,8,1024]{3,1,0,2:T(4,128)S(1)}, u32[]{:S(2)}, u32[]{:S(2)}) async-start(f32[2,4,8,1024]{3,1,0,2:T(4,128)} %reshape.424), calls=%async_computation.6 | async-start | bytes 524288 | tf_op jit(solution)/shard_map/all_to_all | solution.py:51
  135.4 20.6 %all-to-all-start.2 = ((f32[2,4,8,1024]{3,1,0,2:T(4,128)}), f32[2,4,8,1024]{3,1,0,2:T(4,128)S(1)}, u32[]{:S(2)}, u32[]{:S(2)}) async-start(f32[2,4,8,1024]{3,1,0,2:T(4,128)} %reshape.422), calls=%async_computation.2 | async-start | bytes 524288 | tf_op jit(solution)/shard_map/all_to_all | solution.py:51
  156.0 20.8 %all-to-all-start.7 = ((bf16[8,2,4096]{2,1,0:T(2,128)(2,1)}), bf16[8,2,4096]{2,1,0:T(2,128)(2,1)S(1)}, u32[]{:S(2)}, u32[]{:S(2)}) async-start(bf16[8,2,4096]{2,1,0:T(2,128)(2,1)} %reshape.435), calls=%async_computation.7 | async-start | bytes 262144 | tf_op jit(solution)/shard_map/all_to_all | solution.py:63
  162.4 19.4 %copy-start.13 = (s32[8,4]{0,1:T(4,128)S(1)}, s32[8,4]{0,1:T(4,128)}, u32[]{:S(2)}) copy-start(s32[8,4]{0,1:T(4,128)} %param.11) | copy-start | bytes 388
  176.7 26.5 %all-to-all-start.3 = ((bf16[8,2,4096]{2,1,0:T(2,128)(2,1)}), bf16[8,2,4096]{2,1,0:T(2,128)(2,1)S(1)}, u32[]{:S(2)}, u32[]{:S(2)}) async-start(bf16[8,2,4096]{2,1,0:T(2,128)(2,1)} %reshape.441), calls=%async_computation.3 | async-start | bytes 262144 | tf_op jit(solution)/shard_map/all_to_all | solution.py:63
  201.4 34.8 %collective-permute-start.4 = (bf16[1,8,1,4,256]{4,3,2,1,0:T(4,128)(2,1)S(1)}, bf16[1,8,1,4,256]{4,3,2,1,0:T(4,128)(2,1)S(1)}, u32[]{:S(2)}, u32[]{:S(2)}) collective-permute-start(bf16[1,8,1,4,256]{4,3,2,1,0:T(4,128)(2,1)S(1)} %get-tuple-element.30), channel_id=1, source_target_pairs={{0,8},{8,16},{16,24},{24,32},{32,40},{40,48},{48,56},{56,64},{64,7... | collective-permute-start | bytes 49160 | tf_op jit(solution)/shard_map/ppermute | solution.py:20
  229.6 6.7 collective-permute-start.5
  230.9 11.9 %collective-permute-start = (bf16[1,8,1,4,256]{4,3,2,1,0:T(4,128)(2,1)S(1)}, bf16[1,8,1,4,256]{4,3,2,1,0:T(4,128)(2,1)S(1)}, u32[]{:S(2)}, u32[]{:S(2)}) collective-permute-start(bf16[1,8,1,4,256]{4,3,2,1,0:T(4,128)(2,1)S(1)} %get-tuple-element.28), channel_id=1, source_target_pairs={{0,8},{8,16},{16,24},{24,32},{32,40},{40,48},{48,56},{56,64},{64,7... | collective-permute-start | bytes 49160 | tf_op jit(solution)/shard_map/ppermute | solution.py:20
  234.9 8.0 %collective-permute-start.1 = (bf16[1,8,1,4,256]{4,3,2,1,0:T(4,128)(2,1)S(1)}, bf16[1,8,1,4,256]{4,3,2,1,0:T(4,128)(2,1)S(1)}, u32[]{:S(2)}, u32[]{:S(2)}) collective-permute-start(bf16[1,8,1,4,256]{4,3,2,1,0:T(4,128)(2,1)S(1)} %get-tuple-element.27), channel_id=1, source_target_pairs={{8,0},{16,8},{24,16},{32,24},{40,32},{48,40},{56,48},{64,56},{72,6... | collective-permute-start | bytes 49160 | tf_op jit(solution)/shard_map/ppermute | solution.py:21
  236.5 12.8 %collective-permute-start.6 = (bf16[1,8,10,1,256]{4,3,2,1,0:T(2,128)(2,1)S(1)}, bf16[1,8,10,1,256]{4,3,2,1,0:T(2,128)(2,1)S(1)}, u32[]{:S(2)}, u32[]{:S(2)}) collective-permute-start(bf16[1,8,10,1,256]{4,3,2,1,0:T(2,128)(2,1)S(1)} %get-tuple-element.25), channel_id=1, source_target_pairs={{0,1},{1,2},{2,3},{3,4},{4,5},{5,6},{6,7},{8,9},{9,10},{10,11},{11... | collective-permute-start | bytes 122888 | tf_op jit(solution)/shard_map/ppermute | solution.py:20
  240.9 8.4 %collective-permute-start.7 = (bf16[1,8,10,1,256]{4,3,2,1,0:T(2,128)(2,1)S(1)}, bf16[1,8,10,1,256]{4,3,2,1,0:T(2,128)(2,1)S(1)}, u32[]{:S(2)}, u32[]{:S(2)}) collective-permute-start(bf16[1,8,10,1,256]{4,3,2,1,0:T(2,128)(2,1)S(1)} %get-tuple-element.26), channel_id=1, source_target_pairs={{1,0},{2,1},{3,2},{4,3},{5,4},{6,5},{7,6},{9,8},{10,9},{11,10},{12... | collective-permute-start | bytes 122888 | tf_op jit(solution)/shard_map/ppermute | solution.py:21
  243.7 17.3 %collective-permute-start.2 = (bf16[1,8,10,1,256]{4,3,2,1,0:T(2,128)(2,1)}, bf16[1,8,10,1,256]{4,3,2,1,0:T(2,128)(2,1)}, u32[]{:S(2)}, u32[]{:S(2)}) collective-permute-start(bf16[1,8,10,1,256]{4,3,2,1,0:T(2,128)(2,1)} %get-tuple-element.23), channel_id=1, source_target_pairs={{0,1},{1,2},{2,3},{3,4},{4,5},{5,6},{6,7},{8,9},{9,10},{10,11},{11... | collective-permute-start | bytes 122888 | tf_op jit(solution)/shard_map/ppermute | solution.py:20
  247.3 13.7 %collective-permute-start.3 = (bf16[1,8,10,1,256]{4,3,2,1,0:T(2,128)(2,1)}, bf16[1,8,10,1,256]{4,3,2,1,0:T(2,128)(2,1)}, u32[]{:S(2)}, u32[]{:S(2)}) collective-permute-start(bf16[1,8,10,1,256]{4,3,2,1,0:T(2,128)(2,1)} %get-tuple-element.24), channel_id=1, source_target_pairs={{1,0},{2,1},{3,2},{4,3},{5,4},{6,5},{7,6},{9,8},{10,9},{11,10},{12... | collective-permute-start | bytes 122888 | tf_op jit(solution)/shard_map/ppermute | solution.py:21
  261.0 8.0 %copy-start.15 = (pred[8,33]{0,1:T(8,128)(4,1)S(1)}, pred[8,33]{0,1:T(8,128)(4,1)}, u32[]{:S(2)}) copy-start(pred[8,33]{0,1:T(8,128)(4,1)} %constant.88) | copy-start | bytes 796
  262.2 6.8 copy-start.8
  269.0 9.1 %copy-start.2 = (bf16[8,10,6,1,8,33]{0,4,5,2,1,3:T(8,128)(2,1)S(1)}, bf16[8,10,6,1,8,33]{0,4,5,2,1,3:T(8,128)(2,1)}, u32[]{:S(2)}) copy-start(bf16[8,10,6,1,8,33]{0,4,5,2,1,3:T(8,128)(2,1)} %copy.347) | copy-start | bytes 760324
  269.0 9.1 %copy-start.14 = (bf16[8,16,3,3,3]{1,0,4,3,2:T(8,128)(2,1)S(1)}, bf16[8,16,3,3,3]{1,0,4,3,2:T(8,128)(2,1)}, u32[]{:S(2)}) copy-start(bf16[8,16,3,3,3]{1,0,4,3,2:T(8,128)(2,1)} %param.9) | copy-start | bytes 20740
  296.9 122.3 %collective-permute-start.12 = (bf16[1,16,1,4,256]{4,1,3,0,2:T(8,128)(2,1)}, bf16[1,16,1,4,256]{4,1,3,0,2:T(8,128)(2,1)}, u32[]{:S(2)}, u32[]{:S(2)}) collective-permute-start(bf16[1,16,1,4,256]{4,1,3,0,2:T(8,128)(2,1)} %slice_bitcast_fusion.4), channel_id=1, source_target_pairs={{0,8},{8,16},{16,24},{24,32},{32,40},{40,48},{48,56},{56,64},{64,7... | collective-permute-start | bytes 98312 | tf_op jit(solution)/shard_map/ppermute | solution.py:20
  303.2 116.0 %collective-permute-start.13 = (bf16[1,16,1,4,256]{4,1,3,0,2:T(8,128)(2,1)}, bf16[1,16,1,4,256]{4,1,3,0,2:T(8,128)(2,1)}, u32[]{:S(2)}, u32[]{:S(2)}) collective-permute-start(bf16[1,16,1,4,256]{4,1,3,0,2:T(8,128)(2,1)} %slice_bitcast_fusion.3), channel_id=1, source_target_pairs={{8,0},{16,8},{24,16},{32,24},{40,32},{48,40},{56,48},{64,56},{72,6... | collective-permute-start | bytes 98312 | tf_op jit(solution)/shard_map/ppermute | solution.py:21
  305.2 12.1 %copy-start.4 = (bf16[8,10,6,1,7,1]{5,4,2,1,0,3:T(8,128)(2,1)S(1)}, bf16[8,10,6,1,7,1]{5,4,2,1,0,3:T(8,128)(2,1)}, u32[]{:S(2)}) copy-start(bf16[8,10,6,1,7,1]{5,4,2,1,0,3:T(8,128)(2,1)} %get-tuple-element.12) | copy-start | bytes 20164
  306.7 13.5 %collective-permute-start.8 = (bf16[1,16,1,4,256]{4,1,3,0,2:T(8,128)(2,1)S(1)}, bf16[1,16,1,4,256]{4,1,3,0,2:T(8,128)(2,1)S(1)}, u32[]{:S(2)}, u32[]{:S(2)}) collective-permute-start(bf16[1,16,1,4,256]{4,1,3,0,2:T(8,128)(2,1)S(1)} %slice_bitcast_fusion.6), channel_id=1, source_target_pairs={{0,8},{8,16},{16,24},{24,32},{32,40},{40,48},{48,56},{56,64},{64,7... | collective-permute-start | bytes 98312 | tf_op jit(solution)/shard_map/ppermute | solution.py:20
  311.2 9.1 %collective-permute-start.9 = (bf16[1,16,1,4,256]{4,1,3,2,0:T(8,128)(2,1)S(1)}, bf16[1,16,1,4,256]{4,1,3,2,0:T(8,128)(2,1)S(1)}, u32[]{:S(2)}, u32[]{:S(2)}) collective-permute-start(bf16[1,16,1,4,256]{4,1,3,2,0:T(8,128)(2,1)S(1)} %slice_bitcast_fusion.5), channel_id=1, source_target_pairs={{8,0},{16,8},{24,16},{32,24},{40,32},{48,40},{56,48},{64,56},{72,6... | collective-permute-start | bytes 98312 | tf_op jit(solution)/shard_map/ppermute | solution.py:21
  320.3 16.8 %collective-permute-start.10 = (bf16[1,16,10,1,256]{4,1,3,2,0:T(8,128)(2,1)S(1)}, bf16[1,16,10,1,256]{4,1,3,2,0:T(8,128)(2,1)S(1)}, u32[]{:S(2)}, u32[]{:S(2)}) collective-permute-start(bf16[1,16,10,1,256]{4,1,3,2,0:T(8,128)(2,1)S(1)} %get-tuple-element.17), channel_id=1, source_target_pairs={{0,1},{1,2},{2,3},{3,4},{4,5},{5,6},{6,7},{8,9},{9,10},{10,11},{11... | collective-permute-start | bytes 245768 | tf_op jit(solution)/shard_map/ppermute | solution.py:20
  324.8 12.3 %collective-permute-start.11 = (bf16[1,16,10,1,256]{4,1,3,2,0:T(8,128)(2,1)S(1)}, bf16[1,16,10,1,256]{4,1,3,2,0:T(8,128)(2,1)}, u32[]{:S(2)}, u32[]{:S(2)}) collective-permute-start(bf16[1,16,10,1,256]{4,1,3,2,0:T(8,128)(2,1)S(1)} %get-tuple-element.18), channel_id=1, source_target_pairs={{1,0},{2,1},{3,2},{4,3},{5,4},{6,5},{7,6},{9,8},{10,9},{11,10},{12... | collective-permute-start | bytes 245768 | tf_op jit(solution)/shard_map/ppermute | solution.py:21
  330.7 3.5 copy-start.3
  368.4 58.1 %all-to-all-start.8 = ((f32[32,1,2048]{2,1,0:T(1,128)}), f32[32,1,2048]{2,1,0:T(1,128)S(1)}, u32[]{:S(2)}, u32[]{:S(2)}) async-start(f32[32,1,2048]{2,1,0:T(1,128)} %reshape.443), calls=%async_computation.8 | async-start | bytes 524288 | tf_op jit(solution)/shard_map/all_to_all | solution.py:48
  420.6 61.2 %collective-permute-start.14 = (bf16[1,16,10,1,256]{4,1,3,2,0:T(8,128)(2,1)}, bf16[1,16,10,1,256]{4,1,3,2,0:T(8,128)(2,1)}, u32[]{:S(2)}, u32[]{:S(2)}) collective-permute-start(bf16[1,16,10,1,256]{4,1,3,2,0:T(8,128)(2,1)} %get-tuple-element.13), channel_id=1, source_target_pairs={{0,1},{1,2},{2,3},{3,4},{4,5},{5,6},{6,7},{8,9},{9,10},{10,11},{11... | collective-permute-start | bytes 245768 | tf_op jit(solution)/shard_map/ppermute | solution.py:20
  424.5 57.3 %collective-permute-start.15 = (bf16[1,16,10,1,256]{4,1,3,2,0:T(8,128)(2,1)}, bf16[1,16,10,1,256]{4,1,3,2,0:T(8,128)(2,1)}, u32[]{:S(2)}, u32[]{:S(2)}) collective-permute-start(bf16[1,16,10,1,256]{4,1,3,2,0:T(8,128)(2,1)} %get-tuple-element.14), channel_id=1, source_target_pairs={{1,0},{2,1},{3,2},{4,3},{5,4},{6,5},{7,6},{9,8},{10,9},{11,10},{12... | collective-permute-start | bytes 245768 | tf_op jit(solution)/shard_map/ppermute | solution.py:21
  434.2 24.7 %copy-start.5 = (bf16[8,4,8,33,16]{4,2,3,1,0:T(8,128)(2,1)S(1)}, bf16[8,4,8,33,16]{4,2,3,1,0:T(8,128)(2,1)}, u32[]{:S(2)}) copy-start(bf16[8,4,8,33,16]{4,2,3,1,0:T(8,128)(2,1)} %multiply_convert_fusion) | copy-start | bytes 811012
  446.6 48.2 %all-to-all-start.9 = ((f32[32,1,2048]{2,1,0:T(1,128)}), f32[32,1,2048]{2,1,0:T(1,128)S(1)}, u32[]{:S(2)}, u32[]{:S(2)}) async-start(f32[32,1,2048]{2,1,0:T(1,128)} %reshape.445), calls=%async_computation.9 | async-start | bytes 524288 | tf_op jit(solution)/shard_map/all_to_all | solution.py:52
  498.6 178.5 %all-to-all-start.10 = ((f32[2,4,8,1024]{3,1,0,2:T(4,128)}), f32[2,4,8,1024]{3,1,0,2:T(4,128)S(1)}, u32[]{:S(2)}, u32[]{:S(2)}) async-start(f32[2,4,8,1024]{3,1,0,2:T(4,128)} %reshape.426), calls=%async_computation.10 | async-start | bytes 524288 | tf_op jit(solution)/shard_map/all_to_all | solution.py:51
  504.1 90.1 %copy-start.11 = (f32[16,8,3,3,3]{0,1,4,3,2:T(8,128)S(1)}, f32[16,8,3,3,3]{0,1,4,3,2:T(8,128)}, u32[]{:S(2)}) copy-start(f32[16,8,3,3,3]{0,1,4,3,2:T(8,128)} %fusion.52) | copy-start | bytes 41476
  504.1 173.3 %copy-start.9 = (f32[1,2,32,32]{3,2,1,0:T(8,128)S(1)}, f32[1,2,32,32]{3,2,1,0:T(8,128)}, u32[]{:S(2)}) copy-start(f32[1,2,32,32]{3,2,1,0:T(8,128)} %get-tuple-element.31) | copy-start | bytes 24580
  504.1 173.3 %copy-start.10 = (f32[1,2,32,32]{3,2,1,0:T(8,128)S(1)}, f32[1,2,32,32]{3,2,1,0:T(8,128)}, u32[]{:S(2)}) copy-start(f32[1,2,32,32]{3,2,1,0:T(8,128)} %get-tuple-element.32) | copy-start | bytes 24580
  692.1 9.8 %all-to-all-start.11 = ((bf16[8,2,4096]{2,1,0:T(2,128)(2,1)}), bf16[8,2,4096]{2,1,0:T(2,128)(2,1)S(1)}, u32[]{:S(2)}, u32[]{:S(2)}) async-start(bf16[8,2,4096]{2,1,0:T(2,128)(2,1)} %reshape.447), calls=%async_computation.11 | async-start | bytes 262144 | tf_op jit(solution)/shard_map/all_to_all | solution.py:63
  696.1 26.4 %copy-start.1 = (bf16[16,8,3,3,3]{0,1,4,3,2:T(8,128)(2,1)S(1)}, bf16[16,8,3,3,3]{0,1,4,3,2:T(8,128)(2,1)}, u32[]{:S(2)}) copy-start(bf16[16,8,3,3,3]{0,1,4,3,2:T(8,128)(2,1)} %param.8) | copy-start | bytes 20740
  696.8 24.9 %copy-start.7 = (f32[2,4,8,4,256]{4,3,2,1,0:T(4,128)S(1)}, f32[2,4,8,4,256]{4,3,2,1,0:T(4,128)}, u32[]{:S(2)}) copy-start(f32[2,4,8,4,256]{4,3,2,1,0:T(4,128)} %param.7) | copy-start | bytes 786436
  696.8 24.9 %copy-start.12 = (f32[8,4]{1,0:T(8,128)S(1)}, f32[8,4]{1,0:T(8,128)}, u32[]{:S(2)}) copy-start(f32[8,4]{1,0:T(8,128)} %copy.333) | copy-start | bytes 388
where the time goes:
time: 732 us; the launch traced here: 723 us
  local copies, waits for them, and re-layouts  264 us (36%)
  starting transfers between devices  175 us (24%)
  matrix products  151 us (21%)
  blocking collectives  82.3 us (11%)
  other arithmetic  28 us (4%)
  waiting for transfers between devices  19.7 us (3%)
    unnamed x60, local copies, waits for them, and re-layouts  126 us
    transpose x2, matrix products, kernel_gradient(): return summed.transpose(1, 0, 2, 3, 4)  113 us
    psum x1, blocking collectives, local(): summed_in, summed_out = lax.psum((local_in, local_out), ('gy', 'gz'))  82.3 us
    all_to_all x3, starting transfers between devices, spectral(): lax.all_to_all(flattened, 'gy', split_axis=3, concat_axis=2, tiled=True)  62.5 us
    all_to_all x3, starting transfers between devices, spectral(): lax.all_to_all(transformed_y, 'gy', split_axis=2, concat_axis=3, tiled=True)  36.1 us
    ppermute x8, starting transfers between devices, extended(): before = lax.ppermute(last, axis, up)  31.5 us
    conv_general_dilated x3, matrix products, convolve(): lax.conv_general_dilated(padded, kernel, (1, 1, 1), ((0, 0), (0, 0), (1,...  27.8 us
    conv_general_dilated x12, local copies, waits for them, and re-layouts, convolve(): lax.conv_general_dilated(padded, kernel, (1, 1, 1), ((0, 0), (0, 0), (1,...  25.1 us
  transfers between devices with their start and end apart: 28, of which 4 were waited for; matrix products, arithmetic and copies ran while one was open for 49% of the time, Pallas kernels for 0%

commit v1 on v0

v1 whole, which is shorter than its diff:
```python
import functools
import math

import jax
import jax.numpy as jnp
import numpy as np
from jax import lax
from jax.experimental import pallas as pl
from jax.experimental.pallas import tpu as pltpu
from jax.sharding import PartitionSpec as P

BF = jnp.bfloat16
F32 = jnp.float32
NT = (((1,), (1,)), ((), ()))
roll = pltpu.roll


def mm(a, b):
    return jnp.dot(a, b, preferred_element_type=F32)


def mm_nt(a, b):
    return lax.dot_general(a, b, NT, preferred_element_type=F32)


def tables():
    z_l, pc, y_l = np.meshgrid(np.arange(4), np.arange(8), np.arange(8), indexing="ij")
    qy = np.zeros((256, 256), np.float32)
    qy[(y_l * 32 + z_l * 8 + pc).ravel(), (z_l * 64 + pc * 8 + y_l).ravel()] = 1
    m, big = np.meshgrid(np.arange(16), np.arange(16), indexing="ij")
    px = np.zeros((256, 256), np.float32)
    px[(m * 16 + big).ravel(), (16 * big + m).ravel()] = 1
    b, f, h, y = np.meshgrid(np.arange(16), np.arange(2), np.arange(2), np.arange(8), indexing="ij")
    ps = np.zeros((512, 512), np.float32)
    ps[(b * 32 + f * 16 + h * 8 + y).ravel(), (y * 64 + h * 32 + f * 16 + b).ravel()] = 1
    b, h, y = np.meshgrid(np.arange(16), np.arange(2), np.arange(8), indexing="ij")
    pb = np.zeros((256, 256), np.float32)
    pb[(y * 32 + h * 16 + b).ravel(), (b * 16 + h * 8 + y).ravel()] = 1
    ky = (128 * h + 8 * b + y).ravel()
    theta = 2 * np.pi * ((np.arange(256)[:, None] * ky[None, :]) % 256) / 256
    wy = np.concatenate([np.cos(theta), np.sin(theta)], 0) / 16
    j, z_l, c = np.meshgrid(np.arange(8), np.arange(4), np.arange(4), indexing="ij")
    kz = (4 * j + z_l).ravel()
    row = (j * 32 + z_l * 8 + c).ravel()
    col = c.ravel()
    mz = np.zeros((512, 256), np.float64)
    for z in range(32):
        phi = 2 * np.pi * ((kz * z) % 32) / 32
        cs, sn = np.cos(phi) / math.sqrt(32), np.sin(phi) / math.sqrt(32)
        re, im = z * 8 + col, z * 8 + 4 + col
        mz[row, re] = cs
        mz[row + 4, re] = -sn
        mz[row, im] = sn
        mz[row + 4, im] = cs
        mz[256 + row, re] = -sn
        mz[256 + row + 4, re] = -cs
        mz[256 + row, im] = cs
        mz[256 + row + 4, im] = -sn
    out = {"qy": qy, "px": px, "ps": ps, "pb": pb, "wy": wy, "mz": mz, "qyt": qy.T, "pxt": px.T}
    out["wyt"] = np.concatenate([wy[:256].T, wy[256:].T], 1)
    out["mzt"] = np.concatenate([mz[:256].T, mz[256:].T], 1)
    high = {k: v.astype(np.float32).astype(BF) for k, v in out.items()}
    for k in ("wy", "mz"):
        low = (out[k] - high[k].astype(np.float64)).astype(np.float32).astype(BF)
        high[k] = np.stack([high[k], low])
    return high


NAMES = ("qy", "px", "ps", "pb", "wy", "mz", "wyt", "mzt", "qyt", "pxt")


def pack(x, qy, px):
    u = mm(qy, x.astype(BF)).astype(BF)
    return mm_nt(px, u).astype(BF)


def unpack(a, qyt, pxt):
    u = mm(pxt, a).astype(BF)
    return mm_nt(qyt, u)


def swap_blocks(parts):
    parts = list(parts)
    block = lax.broadcasted_iota(jnp.int32, parts[0].shape, 1) // 32
    for bit in (1, 2, 4):
        low = (block & bit) == 0
        for j in range(8):
            if not j & bit:
                a, b = parts[j], parts[j | bit]
                parts[j] = jnp.where(low, a, roll(b, 32 * bit, 1))
                parts[j | bit] = jnp.where(low, roll(a, 256 - 32 * bit, 1), b)
    return parts


def to_volume(d, wy, mz):
    cs = mm(wy[0], d) + mm(wy[1], d)
    cs = jnp.concatenate([cs[:256], cs[256:]], axis=1)
    high = cs.astype(BF)
    low = (cs - high.astype(F32)).astype(BF)
    return mm(high, mz[0]) + (mm(high, mz[1]) + mm(low, mz[0]))


def from_volume(v, wyt, mzt):
    e = mm(v.astype(BF), mzt).astype(BF)
    return mm(wyt, jnp.concatenate([e[:, :256], e[:, 256:]], axis=0)).astype(BF)


def shifted(v, u):
    if u == 0:
        return v
    row = lax.broadcasted_iota(jnp.int32, v.shape, 0)
    n = v.shape[0]
    if u == 1:
        return jnp.where(row == n - 1, 0.0, roll(v, n - 1, 0))
    return jnp.where(row == 0, 0.0, roll(v, 1, 0))


def band_rows(w, pair):
    lane = lax.broadcasted_iota(jnp.int32, (16, 512), 1)
    row = lax.broadcasted_iota(jnp.int32, (16, 512), 0)
    u = 2 * pair + row // 8 - lane // 16
    wide = [jnp.concatenate([k] * 4, axis=1) for k in w]
    zero = jnp.zeros((16, 512), F32)
    return jnp.where(u == -1, wide[0], jnp.where(u == 0, wide[1], jnp.where(u == 1, wide[2], zero)))


def band_sums(g):
    zp = lax.broadcasted_iota(jnp.int32, (16, 256), 1) // 8
    acc = [jnp.zeros((16, 256), F32) for _ in range(3)]
    for z in range(32):
        t = zp - z
        acc[z % 3] = jnp.where((t >= -1) & (t <= 1), g[z * 16:(z + 1) * 16], acc[z % 3])
    out = []
    for u in (-1, 0, 1):
        z = zp - u
        r = (z + 3) % 3
        s = jnp.where(r == 0, acc[0], jnp.where(r == 1, acc[1], acc[2]))
        s = jnp.where((z >= 0) & (z < 32), s, 0.0)
        s = s[:, :128] + s[:, 128:]
        for step in (64, 32, 16, 8):
            s = s + roll(s, step, 1)
        out.append(s)
    return out


def gates(hidden, back_active):
    gate = jax.nn.sigmoid(hidden)
    return hidden * gate, back_active * gate * (1.0 + hidden * (1.0 - gate))


def kernel(kspace, cotangent, factor, wt, qy, px, ps, pb, wy, mz, wyt, mzt, qyt, pxt,
           out, grads,
           a1, r1, s2, r2, plane, halo, fcat, band, zt, bh, send_p, recv_p, s3, r3, s4, r4, gr, ga, gs, gb, gt, gc,
           sem1, sem2, semh, semp, sem3, sem4, semg1, semg2, semg3):
    g = lax.axis_index("gy")
    j = lax.axis_index("gz")
    h, b = g // 16, g % 16
    m = h * 8 + j

    def dev1(p):
        return ((p // 8) * 16 + b, p % 8)

    def dev2(p):
        return (h * 16 + p, j)

    def at_x(p):
        mm_, bb = p % 16, p // 16
        return ((mm_ // 8) * 16 + bb, mm_ % 8)

    x = b * 16 + m
    right = at_x((x + 1) % 256)
    left = at_x((x + 255) % 256)

    barrier = pltpu.get_barrier_semaphore()

    def greet(d, carry):
        pl.semaphore_signal(barrier, inc=1, device_id=dev1((m + d) % 16), device_id_type=pl.DeviceIdType.MESH)
        pl.semaphore_signal(barrier, inc=1, device_id=dev2((b + d) % 16), device_id_type=pl.DeviceIdType.MESH)
        return carry

    lax.fori_loop(1, 16, greet, 0)
    pl.semaphore_signal(barrier, inc=1, device_id=right, device_id_type=pl.DeviceIdType.MESH)
    pl.semaphore_signal(barrier, inc=1, device_id=left, device_id_type=pl.DeviceIdType.MESH)

    def remote(src, dst, sems, i, device):
        return pltpu.make_async_remote_copy(
            src_ref=src, dst_ref=dst, send_sem=sems.at[0, i], recv_sem=sems.at[1, i],
            device_id=device, device_id_type=pl.DeviceIdType.MESH)

    def send_all(me, dev, src, dst, sems):
        def step(d, carry):
            p = (me + d) % 16
            remote(src(p), dst(me), sems, d, dev(p)).start()
            return carry
        lax.fori_loop(1, 16, step, 0)

    def wait_all(me, dev, src, dst, sems):
        def step(d, carry):
            p = (me + d) % 16
            q = (me + 16 - d) % 16
            remote(src(p), dst(q), sems, d, dev(p)).wait_send()
            remote(src(p), dst(q), sems, d, dev(p)).wait_recv()
            return carry
        lax.fori_loop(1, 16, step, 0)

    for f, field in enumerate((kspace, cotangent)):
        rows = jnp.concatenate([field[:, z, :] for z in range(4)], axis=0)
        a1[:, f] = pack(rows, qy[...], px[...]).reshape(16, 16, 256)

    pl.semaphore_wait(barrier, 32)

    ex1 = (m, dev1, lambda p: a1.at[p], lambda p: r1.at[p], sem1)
    send_all(*ex1)
    r1[m] = a1[m]

    def build(t, carry):
        w = [wt[t, u] for u in range(3)]
        for pair in range(16):
            rows_at = pl.multiple_of(t * 256 + pair * 16, 16)
            band[pl.ds(rows_at, 16), :] = band_rows(w, pair).astype(BF)
        return carry

    lax.fori_loop(0, 18, build, 0)
    wait_all(*ex1)

    parts = [jnp.concatenate([r1[k].reshape(32, 256), r1[8 + k].reshape(32, 256)], axis=0).astype(F32) for k in range(8)]
    whole = jnp.concatenate(swap_blocks(parts), axis=0).astype(BF)
    s2[...] = mm(ps[...], whole).astype(BF).reshape(16, 2, 16, 256)
    ex2 = (b, dev2, lambda p: s2.at[p], lambda p: r2.at[:, p], sem2)
    send_all(*ex2)
    r2[:, b] = s2[b]
    wait_all(*ex2)

    for f in range(2):
        v = to_volume(r2[f].reshape(256, 256), wy[...], mz[...])
        plane[f] = (v if f == 0 else -v).astype(BF)

    def halo_copies(f):
        return (remote(plane.at[f], halo.at[0, f], semh, f, right),
                remote(plane.at[f], halo.at[1, f], semh, 2 + f, left))

    for f in range(2):
        for c in halo_copies(f):
            c.start()

    def lay(f, ux, v):
        for uy in (-1, 0, 1):
            tap = (ux + 1) * 3 + uy + 1
            fcat[f, :, tap * 256:(tap + 1) * 256] = shifted(v, uy).astype(BF)

    for f in range(2):
        lay(f, 0, plane[f].astype(F32))
    has_left = jnp.where(x > 0, 1.0, 0.0)
    has_right = jnp.where(x < 255, 1.0, 0.0)
    for f in range(2):
        for c in halo_copies(f):
            c.wait()
        lay(f, -1, halo[0, f].astype(F32) * has_left)
        lay(f, 1, halo[1, f].astype(F32) * has_right)

    hidden = mm(fcat[0], band[0:2304, :])
    back_active = mm(fcat[1], band[2304:4608, :])
    active, back_hidden = gates(hidden, back_active)
    zt[0] = back_hidden.T.astype(BF)
    zt[1] = active.T.astype(BF)
    for uy in (-1, 0, 1):
        bh[uy + 1] = shifted(back_hidden, -uy).astype(BF)

    def share(ux):
        total = None
        for uy in (-1, 0, 1):
            tap = (ux + 1) * 3 + uy + 1
            v = mm_nt(bh[uy + 1], band[tap * 256:(tap + 1) * 256, :])
            total = v if total is None else total + v
        return total

    share_copies = (remote(send_p.at[0], recv_p.at[0], semp, 0, right),
                    remote(send_p.at[1], recv_p.at[1], semp, 1, left))
    send_p[0] = share(1).astype(BF)
    share_copies[0].start()
    send_p[1] = share(-1).astype(BF)
    share_copies[1].start()
    own = share(0)
    for c in share_copies:
        c.wait()
    back_image = own + recv_p[0].astype(F32) * has_left + recv_p[1].astype(F32) * has_right

    s3[...] = from_volume(back_image, wyt[...], mzt[...]).reshape(16, 16, 256)
    ex3 = (b, dev2, lambda p: s3.at[p], lambda p: r3.at[p], sem3)
    send_all(*ex3)
    r3[b] = s3[b]

    gr[...] = jnp.zeros_like(gr)
    slot = lax.broadcasted_iota(jnp.int32, (16, 128), 1) // 8
    for f in range(2):
        for tap in range(9):
            gm = mm(zt[f], fcat[f, :, tap * 256:(tap + 1) * 256])
            for u, s in enumerate(band_sums(gm)):
                k = (f * 9 + tap) * 3 + u
                tile = slice((k // 7) * 16, (k // 7) * 16 + 16)
                gr[tile, :] = jnp.where(slot == k % 7, s, gr[tile, :])
    exg1 = (m, dev1, lambda p: gr.at[pl.ds(pl.multiple_of(p * 8, 8), 8)], lambda p: ga.at[p], semg1)
    send_all(*exg1)
    ga[m] = gr[pl.ds(pl.multiple_of(m * 8, 8), 8), :]

    wait_all(*ex3)
    rows = mm(pb[...], r3[...].reshape(256, 256))
    parts = swap_blocks([rows[k * 32:(k + 1) * 32] for k in range(8)])
    for k in range(8):
        v = parts[k].astype(BF)
        s4[k] = v[:16]
        s4[8 + k] = v[16:]
    ex4 = (m, dev1, lambda p: s4.at[p], lambda p: r4.at[p], sem4)
    send_all(*ex4)
    r4[m] = s4[m]

    wait_all(*exg1)
    gs[...] = jnp.sum(ga[...], axis=0)
    exg2 = (b, dev2, lambda p: gs, lambda p: gb.at[p], semg2)
    send_all(*exg2)
    gb[b] = gs[...]

    wait_all(*ex4)
    spectrum = unpack(r4[...].reshape(256, 256), qyt[...], pxt[...])
    for z in range(4):
        rows = cotangent[:, z, :]
        scaled = rows * factor[z][:, :1]
        out[:, z, :] = rows - scaled + spectrum[z * 64:(z + 1) * 64]

    wait_all(*exg2)
    gt[...] = jnp.sum(gb[...], axis=0)
    exg3 = (m, dev1, lambda p: gt, lambda p: gc.at[p], semg3)
    send_all(*exg3)
    gc[m] = gt[...]
    wait_all(*exg3)
    grads[...] = gc[...]


def local(kspace, cotangent, weight_in, weight_out, consistency_weight, sampling_mask):
    const = tables()
    w_in = weight_in.transpose(4, 2, 3, 1, 0)
    w_out = jnp.flip(weight_out, (2, 3, 4)).transpose(4, 2, 3, 0, 1)
    wt = jnp.stack([w_in, w_out]).reshape(18, 3, 8, 16).astype(F32)
    wt = jnp.tile(wt, (1, 1, 2, 8))
    factor = consistency_weight[0] * sampling_mask.astype(F32)
    factor = jnp.broadcast_to(factor.T[:, None, :, None], (4, 8, 8, 128)).reshape(4, 64, 128)
    vmem = pl.BlockSpec(memory_space=pltpu.VMEM)

    def scratch(*shape, kind=BF):
        return pltpu.VMEM(shape, kind)

    def sems(n):
        return pltpu.SemaphoreType.DMA((2, n))

    out, grads = pl.pallas_call(
        kernel,
        out_shape=(jax.ShapeDtypeStruct((64, 4, 256), F32), jax.ShapeDtypeStruct((16, 8, 128), F32)),
        in_specs=[vmem] * 14,
        out_specs=(vmem, vmem),
        scratch_shapes=[
            scratch(16, 2, 16, 256), scratch(16, 2, 16, 256),
            scratch(16, 2, 16, 256), scratch(2, 16, 16, 256),
            scratch(2, 256, 256), scratch(2, 2, 256, 256),
            scratch(2, 256, 2304), scratch(4608, 512),
            scratch(2, 512, 256), scratch(3, 256, 512),
            scratch(2, 256, 256), scratch(2, 256, 256),
            scratch(16, 16, 256), scratch(16, 16, 256),
            scratch(16, 16, 256), scratch(16, 16, 256),
            scratch(128, 128, kind=F32), scratch(16, 8, 128, kind=F32), scratch(8, 128, kind=F32),
            scratch(16, 8, 128, kind=F32), scratch(8, 128, kind=F32), scratch(16, 8, 128, kind=F32),
            sems(16), sems(16), sems(4), sems(2), sems(16), sems(16), sems(16), sems(16), sems(16),
        ],
        compiler_params=pltpu.CompilerParams(
            collective_id=0, has_side_effects=True, vmem_limit_bytes=48 * 1024 * 1024),
        name="cascade",
    )(kspace.reshape(64, 4, 256), cotangent.reshape(64, 4, 256), factor, wt, *[jnp.asarray(const[k]) for k in NAMES])

    blocks = grads.reshape(8, 16, 16, 8)[:, :, :7].transpose(0, 2, 1, 3).reshape(56, 16, 8)[:54]
    blocks = blocks.reshape(2, 3, 3, 3, 16, 8) * (1.0 / math.sqrt(2097152))
    grad_in = blocks[0].transpose(3, 4, 1, 2, 0)
    grad_out = jnp.flip(blocks[1], (0, 1, 2)).transpose(4, 3, 1, 2, 0)
    return out.reshape(kspace.shape), grad_in, grad_out


def solution(mesh):
    placed = P(None, None, "gy", "gz", None)
    return jax.shard_map(
        local,
        mesh=mesh,
        in_specs=(placed, placed, P(), P(), P(), P("gy", "gz")),
        out_specs=(placed, P(), P()),
        check_vma=False,
    )
```

time: 732 us -> 73.9 us (0.10); the launches traced: 723 us -> 73.7 us
  local copies, waits for them, and re-layouts: 264 us -> 11.3 us
  starting transfers between devices: 175 us -> 0 us
  matrix products: 151 us -> 0 us
  blocking collectives: 82.3 us -> 0 us
  Pallas kernels: 0 us -> 59.9 us
  other arithmetic: 28 us -> 0.88 us
  waiting for transfers between devices: 19.7 us -> 0 us
    all_to_all x12 -> x0, starting transfers between devices: 130 us -> none  [the longest x3 62.5 us: spectral(): lax.all_to_all(flattened, 'gy', split_axis=3, concat_axis=2, tiled=True)]
    unnamed x60 -> x27, local copies, waits for them, and re-layouts: 126 us -> 4.77 us
    transpose x2 -> x0, matrix products: 113 us -> none  [kernel_gradient(): return summed.transpose(1, 0, 2, 3, 4)]
    psum x1 -> x0, blocking collectives: 82.3 us -> none  [local(): summed_in, summed_out = lax.psum((local_in, local_out), ('gy', 'gz'))]
    pallas_call x0 -> x1, Pallas kernels: none -> 59.9 us  [local(): pl.pallas_call(kernel, out_shape=(jax.ShapeDtypeStruct((64, 4, 256), F32)...]
    convert_element_type x22 -> x1, local copies, waits for them, and re-layouts: 48.3 us -> 0.02 us  [local(): wt = jnp.stack([w_in, w_out]).reshape(18, 3, 8, 16).astype(F32)]
    ppermute x16 -> x0, starting transfers between devices: 44.3 us -> none  [the longest x8 31.5 us: extended(): before = lax.ppermute(last, axis, up)]
    all_to_all x19 -> x0, local copies, waits for them, and re-layouts: 34 us -> none  [the longest x3 17.4 us: spectral(): lax.all_to_all(as_sent(transformed_z), 'gz', split_axis=3, concat_axis=2,...]
  transfers between devices with their start and end apart: 28 -> 0, of which waited for: 4 -> 0; matrix products, arithmetic and copies ran while one was open for 49% -> 0% of each run, Pallas kernels for 0% -> 0%
where the time goes in v1:
time: 73.9 us; the launch traced here: 73.7 us
  Pallas kernels  59.9 us (81%)
  local copies, waits for them, and re-layouts  11.3 us (15%)
  between operations  1.52 us (2%)
  other arithmetic  0.88 us (1%)
    pallas_call x1, Pallas kernels, local(): pl.pallas_call(kernel, out_shape=(jax.ShapeDtypeStruct((64, 4, 256), F32)...  59.9 us
    unnamed x27, local copies, waits for them, and re-layouts  4.77 us
    another operation x2, local copies, waits for them, and re-layouts, local(): wt = jnp.tile(wt, (1, 1, 2, 8))  4.71 us

profile of v1, /device:TPU:1, one launch (start us, length us, event | category | flops | bytes accessed | tf_op | source)
XLA Modules:
  0.0 73.7 jit_solution(11978865065866101449)
XLA Ops:
  0.6 0.8 %reverse_bitcast_fusion.1 = bf16[1,3,3,3,8,16]{5,4,1,3,2,0:T(8,128)(2,1)S(1)} fusion(bf16[8,16,3,3,3]{1,0,4,3,2:T(8,128)(2,1)} %param.19), kind=kLoop, calls=%fused_computation.4 | loop fusion | bytes 13824 | tf_op jit(solution)/shard_map/stack | solution.py:343
  1.5 0.8 %maximum_convert_fusion = f32[2,3,3,3,8,16]{5,4,1,3,2,0:T(8,128)S(1)} fusion(bf16[1,3,3,3,8,16]{5,4,1,3,2,0:T(8,128)(2,1)S(1)} %reverse_bitcast_fusion.1, bf16[1,3,3,3,8,16]{5,4,1,3,2,0:T(8,128)(2,1)} %bitcast.33), kind=kLoop, calls=%fused_computation.2 | loop fusion | flops 13824 | bytes 41472 | tf_op jit(solution)/shard_map/convert_element_type | solution.py:343
  2.3 0.0 copy-start.11
  2.3 0.0 copy-start
  2.4 0.0 copy-start.1
  2.4 0.0 copy-start.2
  2.4 0.0 copy-start.3
  2.4 0.0 copy-start.4
  2.4 0.0 copy-start.5
  2.4 0.0 copy-start.6
  2.4 0.0 copy-start.7
  2.4 2.2 %tile.4 = f32[18,3,2,8,8,16]{5,4,3,2,1,0:T(8,128)} broadcast(f32[18,3,8,16]{3,2,1,0:T(8,128)S(1)} %bitcast.30), dimensions={0,1,3,5} | broadcast | bytes 470016 | tf_op jit(solution)/shard_map/tile | solution.py:344
  4.7 2.5 %tile.10.wt = f32[18,3,16,128]{3,2,1,0:T(8,128)S(1)} reshape(f32[18,3,2,8,8,16]{5,4,3,2,1,0:T(8,128)} %tile.4) | data formatting | bytes 884736 | tf_op jit(solution)/shard_map/tile | solution.py:344
  7.8 0.0 copy-done.11
  7.8 0.1 broadcast_in_dim.11
  7.9 0.1 broadcast_in_dim.12.factor
  8.0 0.0 copy-done
  8.0 0.0 copy-done.1
  8.0 0.0 copy-done.2
  8.1 0.0 copy-done.3
  8.1 0.0 copy-done.4
  8.1 0.0 copy-done.5
  8.1 0.0 copy-done.6
  8.1 0.0 copy-done.7
  8.1 0.0 copy-start.8
  8.1 0.9 %copy-done.8 = bf16[256,256]{1,0:T(8,128)(2,1)S(1)} copy-done((bf16[256,256]{1,0:T(8,128)(2,1)S(1)}, bf16[256,256]{1,0:T(8,128)(2,1)}, u32[]{:S(2)}) %copy-start.8) | copy-done | bytes 131096
  9.0 0.0 copy-start.9
  9.0 0.9 %copy-done.9 = bf16[256,256]{1,0:T(8,128)(2,1)S(1)} copy-done((bf16[256,256]{1,0:T(8,128)(2,1)S(1)}, bf16[256,256]{1,0:T(8,128)(2,1)}, u32[]{:S(2)}) %copy-start.9) | copy-done | bytes 131096
  9.9 0.0 copy-start.10
  9.9 0.9 %copy-done.10 = bf16[256,256]{1,0:T(8,128)(2,1)S(1)} copy-done((bf16[256,256]{1,0:T(8,128)(2,1)S(1)}, bf16[256,256]{1,0:T(8,128)(2,1)}, u32[]{:S(2)}) %copy-start.10) | copy-done | bytes 131096
  10.8 59.9 %cascade.1 = (f32[64,4,256]{2,1,0:T(4,128)S(1)}, f32[16,8,128]{2,1,0:T(8,128)S(1)}) custom-call(f32[64,4,256]{2,1,0:T(4,128)S(1)} %bitcast.27, f32[64,4,256]{2,1,0:T(4,128)S(1)} %bitcast.28, f32[4,64,128]{2,1,0:T(8,128)S(1)} %broadcast_in_dim.12.factor, f32[18,3,16,128]{3,2,1,0:T(8,128)S(1)} %tile.10.wt, bf16[256,256]{1,0:T(8,128)(2,1)S(1)} %copy-done.8, ...), custom_call_target="tpu_custom_call" | custom-call | tf_op jit(solution)/shard_map/cascade/pallas_call | solution.py:355
  70.8 0.6 reshape.45
  71.4 0.2 copy.20
  71.7 0.7 copy.22
  72.3 0.7 copy.21
  73.0 0.7 copy.25
  (7 shorter events, 0.1 us)
Async XLA Ops:
  2.3 5.5 %copy-start.11 = (s32[8,4]{0,1:T(4,128)S(1)}, s32[8,4]{0,1:T(4,128)}, u32[]{:S(2)}) copy-start(s32[8,4]{0,1:T(4,128)} %param.21) | copy-start | bytes 388
  2.3 5.7 %copy-start = (bf16[512,512]{1,0:T(8,128)(2,1)S(1)}, bf16[512,512]{1,0:T(8,128)(2,1)}, u32[]{:S(2)}) copy-start(bf16[512,512]{1,0:T(8,128)(2,1)} %constant.22.clone.ps) | copy-start | bytes 1572868
  2.4 5.7 %copy-start.1 = (bf16[2,512,256]{2,1,0:T(8,128)(2,1)S(1)}, bf16[2,512,256]{2,1,0:T(8,128)(2,1)}, u32[]{:S(2)}) copy-start(bf16[2,512,256]{2,1,0:T(8,128)(2,1)} %constant.24.clone.wy) | copy-start | bytes 1572868
  2.4 5.7 %copy-start.2 = (bf16[2,512,256]{2,1,0:T(8,128)(2,1)S(1)}, bf16[2,512,256]{2,1,0:T(8,128)(2,1)}, u32[]{:S(2)}) copy-start(bf16[2,512,256]{2,1,0:T(8,128)(2,1)} %constant.25.clone.mz) | copy-start | bytes 1572868
  2.4 5.7 %copy-start.3 = (bf16[256,256]{1,0:T(8,128)(2,1)S(1)}, bf16[256,256]{1,0:T(8,128)(2,1)}, u32[]{:S(2)}) copy-start(bf16[256,256]{1,0:T(8,128)(2,1)} %constant.21.clone.px.pxt) | copy-start | bytes 393220
  2.4 5.7 %copy-start.4 = (f32[2,4,8,4,256]{4,3,2,1,0:T(4,128)S(1)}, f32[2,4,8,4,256]{4,3,2,1,0:T(4,128)}, u32[]{:S(2)}) copy-start(f32[2,4,8,4,256]{4,3,2,1,0:T(4,128)} %param.16) | copy-start | bytes 786436
  2.4 5.7 %copy-start.5 = (f32[2,4,8,4,256]{4,3,2,1,0:T(4,128)S(1)}, f32[2,4,8,4,256]{4,3,2,1,0:T(4,128)}, u32[]{:S(2)}) copy-start(f32[2,4,8,4,256]{4,3,2,1,0:T(4,128)} %param.17) | copy-start | bytes 786436
  2.4 5.7 %copy-start.6 = (bf16[256,512]{1,0:T(8,128)(2,1)S(1)}, bf16[256,512]{1,0:T(8,128)(2,1)}, u32[]{:S(2)}) copy-start(bf16[256,512]{1,0:T(8,128)(2,1)} %constant.26.clone.wyt) | copy-start | bytes 786436
  2.4 5.7 %copy-start.7 = (bf16[256,512]{1,0:T(8,128)(2,1)S(1)}, bf16[256,512]{1,0:T(8,128)(2,1)}, u32[]{:S(2)}) copy-start(bf16[256,512]{1,0:T(8,128)(2,1)} %constant.27.clone.mzt) | copy-start | bytes 786436
  8.1 0.9 %copy-start.8 = (bf16[256,256]{1,0:T(8,128)(2,1)S(1)}, bf16[256,256]{1,0:T(8,128)(2,1)}, u32[]{:S(2)}) copy-start(bf16[256,256]{1,0:T(8,128)(2,1)} %constant.20.clone.qy) | copy-start | bytes 393220
  9.0 0.9 %copy-start.9 = (bf16[256,256]{1,0:T(8,128)(2,1)S(1)}, bf16[256,256]{1,0:T(8,128)(2,1)}, u32[]{:S(2)}) copy-start(bf16[256,256]{1,0:T(8,128)(2,1)} %constant.23.clone.pb) | copy-start | bytes 393220
  9.9 0.9 %copy-start.10 = (bf16[256,256]{1,0:T(8,128)(2,1)S(1)}, bf16[256,256]{1,0:T(8,128)(2,1)}, u32[]{:S(2)}) copy-start(bf16[256,256]{1,0:T(8,128)(2,1)} %constant.28.clone.qyt) | copy-start | bytes 393220

commit v2 on v1

v2 whole, which is shorter than its diff:
```python
import math

import jax
import jax.numpy as jnp
import numpy as np
from jax import lax
from jax.experimental import pallas as pl
from jax.experimental.pallas import tpu as pltpu
from jax.sharding import PartitionSpec as P

BF = jnp.bfloat16
F32 = jnp.float32
NT = (((1,), (1,)), ((), ()))
roll = pltpu.roll


def mm(a, b):
    return jnp.dot(a, b, preferred_element_type=F32)


def mm_nt(a, b):
    return lax.dot_general(a, b, NT, preferred_element_type=F32)


def tables():
    z_l, pc, y_l = np.meshgrid(np.arange(4), np.arange(8), np.arange(8), indexing="ij")
    qy = np.zeros((256, 256), np.float32)
    qy[(y_l * 32 + z_l * 8 + pc).ravel(), (z_l * 64 + pc * 8 + y_l).ravel()] = 1
    m, big = np.meshgrid(np.arange(16), np.arange(16), indexing="ij")
    px = np.zeros((256, 256), np.float32)
    px[(m * 16 + big).ravel(), (16 * big + m).ravel()] = 1
    b, h, y = np.meshgrid(np.arange(16), np.arange(2), np.arange(8), indexing="ij")
    pb = np.zeros((256, 256), np.float32)
    pb[(y * 32 + h * 16 + b).ravel(), (b * 16 + h * 8 + y).ravel()] = 1
    ky = (128 * h + 8 * b + y).ravel()
    theta = 2 * np.pi * ((np.arange(256)[:, None] * ky[None, :]) % 256) / 256
    wy = np.concatenate([np.cos(theta), np.sin(theta)], 0) / 16
    j, z_l, c = np.meshgrid(np.arange(8), np.arange(4), np.arange(4), indexing="ij")
    kz = (4 * j + z_l).ravel()
    row = (j * 32 + z_l * 8 + c).ravel()
    col = c.ravel()
    mz = np.zeros((512, 256), np.float64)
    for z in range(32):
        phi = 2 * np.pi * ((kz * z) % 32) / 32
        cs, sn = np.cos(phi) / math.sqrt(32), np.sin(phi) / math.sqrt(32)
        re, im = z * 8 + col, z * 8 + 4 + col
        mz[row, re] = cs
        mz[row + 4, re] = -sn
        mz[row, im] = sn
        mz[row + 4, im] = cs
        mz[256 + row, re] = -sn
        mz[256 + row + 4, re] = -cs
        mz[256 + row, im] = cs
        mz[256 + row + 4, im] = -sn
    out = {"qy": qy, "px": px, "pbt": pb.T, "pb": pb, "wy": wy, "mz": mz, "qyt": qy.T, "pxt": px.T}
    out["wyt"] = np.concatenate([wy[:256].T, wy[256:].T], 1)
    out["mzt"] = np.concatenate([mz[:256].T, mz[256:].T], 1)
    high = {k: v.astype(np.float32).astype(BF) for k, v in out.items()}
    low = {k: (out[k] - high[k].astype(np.float64)).astype(np.float32).astype(BF) for k in ("wy", "mz")}
    first = np.concatenate([high["qy"], high["px"], high["pbt"]])
    wide = np.concatenate([high["wyt"], high["mzt"]])
    rest = np.concatenate([high["wy"], low["wy"], high["mz"], low["mz"], high["pb"], high["qyt"], high["pxt"]])
    return first, wide, rest


def pack(x, qy, px):
    u = mm(qy, x.astype(BF)).astype(BF)
    return mm_nt(px, u).astype(BF)


def unpack(a, qyt, pxt):
    u = mm(pxt, a).astype(BF)
    return mm_nt(qyt, u)


def swap_blocks(parts):
    parts = list(parts)
    block = lax.broadcasted_iota(jnp.int32, parts[0].shape, 1) // 32
    for bit in (1, 2, 4):
        low = (block & bit) == 0
        for j in range(8):
            if not j & bit:
                a, b = parts[j], parts[j | bit]
                parts[j] = jnp.where(low, a, roll(b, 32 * bit, 1))
                parts[j | bit] = jnp.where(low, roll(a, 256 - 32 * bit, 1), b)
    return parts


def to_volume(d, wy, mz):
    cs = mm(wy[0], d) + mm(wy[1], d)
    cs = jnp.concatenate([cs[:256], cs[256:]], axis=1)
    high = cs.astype(BF)
    low = (cs - high.astype(F32)).astype(BF)
    return mm(high, mz[0]) + (mm(high, mz[1]) + mm(low, mz[0]))


def from_volume(v, wyt, mzt):
    e = mm(v.astype(BF), mzt).astype(BF)
    return mm(wyt, jnp.concatenate([e[:, :256], e[:, 256:]], axis=0)).astype(BF)


def shifted(v, u):
    if u == 0:
        return v
    row = lax.broadcasted_iota(jnp.int32, v.shape, 0)
    n = v.shape[0]
    if u == 1:
        return jnp.where(row == n - 1, 0.0, roll(v, n - 1, 0))
    return jnp.where(row == 0, 0.0, roll(v, 1, 0))


def band_block(w, start):
    lane = lax.broadcasted_iota(jnp.int32, (16, 128), 1)
    row = lax.broadcasted_iota(jnp.int32, (16, 128), 0)
    u = row // 8 - start - lane // 16
    return jnp.where(u == -1, w[0], jnp.where(u == 0, w[1], jnp.where(u == 1, w[2], 0.0))).astype(BF)


def band_sums(g):
    zp = lax.broadcasted_iota(jnp.int32, (16, 256), 1) // 8
    acc = [jnp.zeros((16, 256), F32) for _ in range(3)]
    for z in range(32):
        t = zp - z
        acc[z % 3] = jnp.where((t >= -1) & (t <= 1), g[z * 16:(z + 1) * 16], acc[z % 3])
    out = []
    for u in (-1, 0, 1):
        z = zp - u
        r = (z + 3) % 3
        s = jnp.where(r == 0, acc[0], jnp.where(r == 1, acc[1], acc[2]))
        s = jnp.where((z >= 0) & (z < 32), s, 0.0)
        s = s[:, :128] + s[:, 128:]
        for step in (64, 32, 16, 8):
            s = s + roll(s, step, 1)
        out.append(s)
    return out


def gates(hidden, back_active):
    gate = jax.nn.sigmoid(hidden)
    return hidden * gate, back_active * gate * (1.0 + hidden * (1.0 - gate))


def kernel(kspace_hbm, cotangent_hbm, mask, weight_in, weight_out, consistency, first_hbm, wide_hbm, rest_hbm,
           out, grad_in, grad_out,
           kspace, cotangent, first, wide, rest, wt, seml,
           a1, r1, s2, r2, planes, band, zt, bh, send_p, recv_p, s3, r3, s4, r4, gr, ga, gs, gb, gt, gc,
           sem1, sem2, semh, semp, sem3, sem4, semg1, semg2, semg3):
    g = lax.axis_index("gy")
    j = lax.axis_index("gz")
    h, b = g // 16, g % 16
    m = h * 8 + j

    def dev1(p):
        return ((p // 8) * 16 + b, p % 8)

    def dev2(p):
        return (h * 16 + p, j)

    def at_x(p):
        mm_, bb = p % 16, p // 16
        return ((mm_ // 8) * 16 + bb, mm_ % 8)

    x = b * 16 + m
    right = at_x((x + 1) % 256)
    left = at_x((x + 255) % 256)

    barrier = pltpu.get_barrier_semaphore()

    def greet(d, carry):
        pl.semaphore_signal(barrier, inc=1, device_id=dev1((m + d) % 16), device_id_type=pl.DeviceIdType.MESH)
        pl.semaphore_signal(barrier, inc=1, device_id=dev2((b + d) % 16), device_id_type=pl.DeviceIdType.MESH)
        return carry

    lax.fori_loop(1, 16, greet, 0)
    pl.semaphore_signal(barrier, inc=1, device_id=right, device_id_type=pl.DeviceIdType.MESH)
    pl.semaphore_signal(barrier, inc=1, device_id=left, device_id_type=pl.DeviceIdType.MESH)

    loads = [pltpu.make_async_copy(src, dst, seml.at[i]) for i, (src, dst) in enumerate((
        (first_hbm, first), (kspace_hbm, kspace), (cotangent_hbm, cotangent), (rest_hbm, rest), (wide_hbm, wide)))]
    for c in loads:
        c.start()
    qy, px, pbt = (first.at[256 * i:256 * (i + 1)] for i in range(3))
    wyt, mzt = (wide.at[256 * i:256 * (i + 1)] for i in range(2))
    wy, wy_low, mz, mz_low = (rest.at[512 * i:512 * (i + 1)] for i in range(4))
    pb, qyt, pxt = (rest.at[2048 + 256 * i:2304 + 256 * i] for i in range(3))

    def remote(src, dst, sems, i, device):
        return pltpu.make_async_remote_copy(
            src_ref=src, dst_ref=dst, send_sem=sems.at[0, i], recv_sem=sems.at[1, i],
            device_id=device, device_id_type=pl.DeviceIdType.MESH)

    def send_all(me, dev, src, dst, sems):
        def step(d, carry):
            p = (me + d) % 16
            remote(src(p), dst(me), sems, d, dev(p)).start()
            return carry
        lax.fori_loop(1, 16, step, 0)

    def wait_all(me, dev, src, dst, sems):
        def step(d, carry):
            p = (me + d) % 16
            q = (me + 16 - d) % 16
            remote(src(p), dst(q), sems, d, dev(p)).wait_recv()
            remote(src(p), dst(q), sems, d, dev(p)).wait_send()
            return carry
        lax.fori_loop(1, 16, step, 0)

    ex1 = [(m, dev1, lambda p, f=f: a1.at[f, p], lambda p, f=f: r1.at[f, p], sem1.at[f]) for f in range(2)]
    ex2 = [(b, dev2, lambda p, f=f: s2.at[f, p], lambda p, f=f: r2.at[f, p], sem2.at[f]) for f in range(2)]
    loads[0].wait()
    for f, field in enumerate((kspace, cotangent)):
        loads[1 + f].wait()
        rows = jnp.concatenate([field[:, z, :] for z in range(4)], axis=0)
        a1[f] = pack(rows, qy[...], px[...]).reshape(16, 16, 256)
        if f == 0:
            pl.semaphore_wait(barrier, 32)
        send_all(*ex1[f])
        r1[f, m] = a1[f, m]

    spread = (lax.broadcasted_iota(jnp.int32, (16, 128), 1) % 16 == lax.broadcasted_iota(jnp.int32, (16, 128), 0)).astype(BF)
    for f, w in enumerate((weight_in, weight_out)):
        wt[216 * f:216 * (f + 1), :] = mm(w[...].astype(F32).reshape(216, 16).astype(BF), spread)

    def build(t, carry):
        f, uy, ux = t // 9, t % 9 // 3, t % 3
        w = []
        for uz in range(3):
            k = uy * 9 + uz * 3 + ux
            k = k + f * (53 - 2 * k)
            block = wt[pl.ds(pl.multiple_of(k * 8, 8), 8), :]
            w.append(jnp.concatenate([block, block], axis=0))
        at = [band_block(w, -2 * i) for i in range(4)]
        before, after = band_block(w, -8), band_block(w, 2)
        zero = jnp.zeros((16, 128), BF)
        for pair in range(16):
            own = pair // 4
            cells = [zero] * 4
            cells[own] = at[pair % 4]
            if pair % 4 == 0 and own > 0:
                cells[own - 1] = before
            if pair % 4 == 3 and own < 3:
                cells[own + 1] = after
            rows_at = pl.multiple_of(t * 256 + pair * 16, 16)
            band[pl.ds(rows_at, 16), :] = jnp.concatenate(cells, axis=1)
        return carry

    lax.fori_loop(0, 18, build, 0)

    for f in range(2):
        wait_all(*ex1[f])
        parts = [jnp.concatenate([r1[f, k], r1[f, 8 + k]], axis=0).astype(F32) for k in range(8)]
        whole = jnp.concatenate(swap_blocks(parts), axis=0).astype(BF)
        s2[f] = mm(pbt[...], whole).astype(BF).reshape(16, 16, 256)
        send_all(*ex2[f])
        r2[f, b] = s2[f, b]

    def halo_copies(f):
        return (remote(planes.at[f, 1], planes.at[f, 0], semh, f, right),
                remote(planes.at[f, 1], planes.at[f, 2], semh, 2 + f, left))

    loads[3].wait()
    loads[4].wait()
    for f in range(2):
        wait_all(*ex2[f])
        v = to_volume(r2[f].reshape(256, 256), (wy[...], wy_low[...]), (mz[...], mz_low[...]))
        planes[f, 1] = (v if f == 0 else -v).astype(BF)
        for c in halo_copies(f):
            c.start()

    has_left = jnp.where(x > 0, 1.0, 0.0)
    has_right = jnp.where(x < 255, 1.0, 0.0)
    convolved = []
    for f in range(2):
        for c in halo_copies(f):
            c.wait()

        @pl.when(x == 0)
        def _():
            planes[f, 0] = jnp.zeros((256, 256), BF)

        @pl.when(x == 255)
        def _():
            planes[f, 2] = jnp.zeros((256, 256), BF)

        cat = jnp.concatenate([planes[f, ux] for ux in range(3)], axis=1)
        total = None
        for uy in (-1, 0, 1):
            row = f * 2304 + (uy + 1) * 768
            v = shifted(mm(cat, band[row:row + 768, :]), uy)
            total = v if total is None else total + v
        convolved.append(total)

    active, back_hidden = gates(*convolved)
    for uy in (-1, 0, 1):
        bh[uy + 1] = shifted(back_hidden, -uy).astype(BF)

    def share(ux):
        total = None
        for uy in (-1, 0, 1):
            row = (uy + 1) * 768 + (ux + 1) * 256
            v = mm_nt(bh[uy + 1], band[row:row + 256, :])
            total = v if total is None else total + v
        return total

    share_copies = (remote(send_p.at[0], recv_p.at[0], semp, 0, right),
                    remote(send_p.at[1], recv_p.at[1], semp, 1, left))
    send_p[0] = share(1).astype(BF)
    share_copies[0].start()
    send_p[1] = share(-1).astype(BF)
    share_copies[1].start()
    own = share(0)

    lane = lax.broadcasted_iota(jnp.int32, (512, 256), 1)
    for f, v in enumerate((back_hidden, active)):
        v = v.T
        zt[f, 0] = jnp.where(lane == 255, 0.0, roll(v, 255, 1)).astype(BF)
        zt[f, 1] = v.astype(BF)
        zt[f, 2] = jnp.where(lane == 0, 0.0, roll(v, 1, 1)).astype(BF)
    gr[...] = jnp.zeros_like(gr)
    slot = lax.broadcasted_iota(jnp.int32, (16, 128), 1) // 8
    for t in range(18):
        gm = mm(zt[t // 9, t % 9 // 3], planes[t // 9, t % 3])
        for u, s in enumerate(band_sums(gm)):
            k = t * 3 + u
            tile = slice((k // 7) * 16, (k // 7) * 16 + 16)
            gr[tile, :] = jnp.where(slot == k % 7, s, gr[tile, :])
    exg1 = (m, dev1, lambda p: gr.at[pl.ds(pl.multiple_of(p * 8, 8), 8)], lambda p: ga.at[p], semg1)
    send_all(*exg1)
    ga[m] = gr[pl.ds(pl.multiple_of(m * 8, 8), 8), :]

    for c in share_copies:
        c.wait()
    back_image = own + recv_p[0].astype(F32) * has_left + recv_p[1].astype(F32) * has_right

    s3[...] = from_volume(back_image, wyt[...], mzt[...]).reshape(16, 16, 256)
    ex3 = (b, dev2, lambda p: s3.at[p], lambda p: r3.at[p], sem3)
    send_all(*ex3)
    r3[b] = s3[b]

    wait_all(*exg1)
    gs[...] = jnp.sum(ga[...], axis=0)
    exg2 = (b, dev2, lambda p: gs, lambda p: gb.at[p], semg2)
    send_all(*exg2)
    gb[b] = gs[...]

    wait_all(*ex3)
    rows = mm(pb[...], r3[...].reshape(256, 256))
    parts = swap_blocks([rows[k * 32:(k + 1) * 32] for k in range(8)])
    for k in range(8):
        v = parts[k].astype(BF)
        s4[k] = v[:16]
        s4[8 + k] = v[16:]
    ex4 = (m, dev1, lambda p: s4.at[p], lambda p: r4.at[p], sem4)
    send_all(*ex4)
    r4[m] = s4[m]

    wait_all(*exg2)
    gt[...] = jnp.sum(gb[...], axis=0)
    exg3 = (m, dev1, lambda p: gt, lambda p: gc.at[p], semg3)
    send_all(*exg3)
    gc[m] = gt[...]

    wait_all(*ex4)
    spectrum = unpack(r4[...].reshape(256, 256), qyt[...], pxt[...])
    factor = mask[...].astype(F32)
    eye = lax.broadcasted_iota(jnp.int32, (8, 8), 0) == lax.broadcasted_iota(jnp.int32, (8, 8), 1)
    for z in range(4):
        rows = cotangent[:, z, :]
        sampled = jnp.sum(jnp.where(eye, factor[z:z + 1], 0.0), axis=1, keepdims=True) * consistency[0]
        scaled = (rows.reshape(8, 8, 256) * sampled[None]).reshape(64, 256)
        out[:, z, :] = rows - scaled + spectrum[z * 64:(z + 1) * 64]

    wait_all(*exg3)
    turned = gc[...].reshape(128, 128).T
    for t in range(8):
        at_front = turned if t == 0 else roll(turned, 128 - 16 * t, 1)
        for slot_at in range(7):
            k = 7 * t + slot_at
            if k < 54:
                f, uy, ux, uz = k // 27, k // 9 % 3, k // 3 % 3, k % 3
                n = uy * 9 + uz * 3 + ux
                block = at_front[slot_at * 8:slot_at * 8 + 8, :16]
                if f == 0:
                    grad_in[n] = block
                else:
                    grad_out[26 - n] = block


def local(kspace, cotangent, weight_in, weight_out, consistency_weight, sampling_mask):
    w_in = weight_in.transpose(2, 3, 4, 1, 0).reshape(27, 8, 16)
    w_out = weight_out.transpose(2, 3, 4, 0, 1).reshape(27, 8, 16)
    vmem = pl.BlockSpec(memory_space=pltpu.VMEM)
    hbm = pl.BlockSpec(memory_space=pltpu.HBM)

    def scratch(*shape, kind=BF):
        return pltpu.VMEM(shape, kind)

    def sems(n):
        return pltpu.SemaphoreType.DMA((2, n))

    grad_shape = jax.ShapeDtypeStruct((27, 8, 16), F32)
    out, grad_in, grad_out = pl.pallas_call(
        kernel,
        out_shape=(jax.ShapeDtypeStruct((64, 4, 256), F32), grad_shape, grad_shape),
        in_specs=[hbm, hbm, vmem, vmem, vmem, pl.BlockSpec(memory_space=pltpu.SMEM), hbm, hbm, hbm],
        out_specs=(vmem, vmem, vmem),
        scratch_shapes=[
            scratch(64, 4, 256, kind=F32), scratch(64, 4, 256, kind=F32),
            scratch(768, 256), scratch(512, 512), scratch(2816, 256), scratch(432, 128, kind=F32),
            pltpu.SemaphoreType.DMA((5,)),
            scratch(2, 16, 16, 256), scratch(2, 16, 16, 256), scratch(2, 16, 16, 256), scratch(2, 16, 16, 256),
            scratch(2, 3, 256, 256), scratch(4608, 512), scratch(2, 3, 512, 256), scratch(3, 256, 512),
            scratch(2, 256, 256), scratch(2, 256, 256),
            scratch(16, 16, 256), scratch(16, 16, 256),
            scratch(16, 16, 256), scratch(16, 16, 256),
            scratch(128, 128, kind=F32), scratch(16, 8, 128, kind=F32), scratch(8, 128, kind=F32),
            scratch(16, 8, 128, kind=F32), scratch(8, 128, kind=F32), scratch(16, 8, 128, kind=F32),
            pltpu.SemaphoreType.DMA((2, 2, 16)), pltpu.SemaphoreType.DMA((2, 2, 16)), sems(4), sems(2), sems(16), sems(16), sems(16), sems(16), sems(16),
        ],
        compiler_params=pltpu.CompilerParams(
            collective_id=0, has_side_effects=True, vmem_limit_bytes=62 * 1024 * 1024),
        name="cascade",
    )(kspace.reshape(64, 4, 256), cotangent.reshape(64, 4, 256), sampling_mask.T, w_in, w_out, consistency_weight, *map(jnp.asarray, tables()))
    scale = 1.0 / math.sqrt(2097152)
    grad_in = (grad_in * scale).reshape(3, 3, 3, 8, 16).transpose(4, 3, 0, 1, 2)
    grad_out = (grad_out * scale).reshape(3, 3, 3, 8, 16).transpose(3, 4, 0, 1, 2)
    return out.reshape(kspace.shape), grad_in, grad_out


def solution(mesh):
    placed = P(None, None, "gy", "gz", None)
    return jax.shard_map(
        local,
        mesh=mesh,
        in_specs=(placed, placed, P(), P(), P(), P("gy", "gz")),
        out_specs=(placed, P(), P()),
        check_vma=False,
    )
```

time: 73.9 us -> 57.5 us (0.78)
  local copies, waits for them, and re-layouts: 11.3 us -> 1.67 us
  Pallas kernels: 59.9 us -> 52.7 us
  other arithmetic: 0.88 us -> 1.65 us
    pallas_call x1, Pallas kernels: 59.9 us -> 52.7 us  [local(): pl.pallas_call(kernel, out_shape=(jax.ShapeDtypeStruct((64, 4, 256), F32)...]
    another operation x3 -> x0, local copies, waits for them, and re-layouts: 5.54 us -> none  [the longest x2 4.71 us: local(): wt = jnp.tile(wt, (1, 1, 2, 8))]
    unnamed x27 -> x1, local copies, waits for them, and re-layouts: 4.77 us -> 1.67 us
    mul x1, other arithmetic: 0.03 us -> 1.65 us  [local(): grad_out * scale]
    convert_element_type x1 -> x0, other arithmetic: 0.85 us -> none  [local(): wt = jnp.stack([w_in, w_out]).reshape(18, 3, 8, 16).astype(F32)]
where the time goes in v2:
time: 57.5 us; the launch traced here: 57.3 us
  Pallas kernels  52.7 us (92%)
  local copies, waits for them, and re-layouts  1.67 us (3%)
  other arithmetic  1.65 us (3%)
  between operations  1.29 us (2%)
    pallas_call x1, Pallas kernels, local(): pl.pallas_call(kernel, out_shape=(jax.ShapeDtypeStruct((64, 4, 256), F32)...  52.7 us
    unnamed x1, local copies, waits for them, and re-layouts  1.67 us
    mul x1, other arithmetic, local(): grad_out * scale  1.65 us

profile of v2, /device:TPU:1, one launch (start us, length us, event | category | flops | bytes accessed | tf_op | source)
XLA Modules:
  0.0 57.3 jit_solution(16090132465680159630)
XLA Ops:
  1.3 52.7 %cascade.1 = (f32[64,4,256]{2,1,0:T(4,128)}, f32[27,8,16]{2,1,0:T(8,128)}, f32[27,8,16]{2,1,0:T(8,128)}) custom-call(f32[64,4,256]{2,1,0:T(4,128)} %bitcast.17, f32[64,4,256]{2,1,0:T(4,128)} %bitcast.18, s32[4,8]{1,0:T(4,128)} %bitcast.23, bf16[27,8,16]{2,1,0:T(8,128)(2,1)} %bitcast.21, bf16[27,8,16]{2,1,0:T(8,128)(2,1)} %bitcast.22, ...), custom_call_target="tpu_custom_call" | custom-call | tf_op jit(solution)/shard_map/cascade/pallas_call | solution.py:402
  54.0 1.7 %broadcast_multiply_fusion = (f32[27,8,16]{2,1,0:T(8,128)}, f32[27,8,16]{2,1,0:T(8,128)}) fusion(f32[27,8,16]{2,1,0:T(8,128)} %get-tuple-element.8, f32[27,8,16]{2,1,0:T(8,128)} %get-tuple-element.7), kind=kLoop, calls=%fused_computation | loop fusion | flops 6912 | bytes 55296 | tf_op jit(solution)/shard_map/mul | solution.py:426
  55.6 1.7 %copy.14 = f32[2,4,8,4,256]{4,3,2,1,0:T(4,128)} copy(f32[2,4,8,4,256]{4,3,2,1,0:T(4,128)} %bitcast.16) | data formatting | bytes 524288

commit v3 on v2

--- a/solution.py
+++ b/solution.py
@@ -22,13 +22,21 @@
     return lax.dot_general(a, b, NT, preferred_element_type=F32)
 
 
+def plane_of(m, b):
+    return b * 16 + m
+
+
+def member_of(x):
+    return x % 16, x // 16
+
+
 def tables():
     z_l, pc, y_l = np.meshgrid(np.arange(4), np.arange(8), np.arange(8), indexing="ij")
     qy = np.zeros((256, 256), np.float32)
     qy[(y_l * 32 + z_l * 8 + pc).ravel(), (z_l * 64 + pc * 8 + y_l).ravel()] = 1
-    m, big = np.meshgrid(np.arange(16), np.arange(16), indexing="ij")
+    m, b = np.meshgrid(np.arange(16), np.arange(16), indexing="ij")
     px = np.zeros((256, 256), np.float32)
-    px[(m * 16 + big).ravel(), (16 * big + m).ravel()] = 1
+    px[(m * 16 + b).ravel(), plane_of(m, b).ravel()] = 1
     b, h, y = np.meshgrid(np.arange(16), np.arange(2), np.arange(8), indexing="ij")
     pb = np.zeros((256, 256), np.float32)
     pb[(y * 32 + h * 16 + b).ravel(), (b * 16 + h * 8 + y).ravel()] = 1
@@ -73,17 +81,25 @@
     return mm_nt(qyt, u)
 
 
-def swap_blocks(parts):
+def swap_four(parts):
     parts = list(parts)
     block = lax.broadcasted_iota(jnp.int32, parts[0].shape, 1) // 32
-    for bit in (1, 2, 4):
+    for bit in (1, 2):
         low = (block & bit) == 0
-        for j in range(8):
+        for j in range(4):
             if not j & bit:
                 a, b = parts[j], parts[j | bit]
                 parts[j] = jnp.where(low, a, roll(b, 32 * bit, 1))
-                parts[j | bit] = jnp.where(low, roll(a, 256 - 32 * bit, 1), b)
+                parts[j | bit] = jnp.where(low, roll(a, 128 - 32 * bit, 1), b)
     return parts
+
+
+def swap_blocks(parts):
+    out = []
+    for y in (0, 128):
+        low, high = (swap_four([p[:, y:y + 128] for p in parts[k:k + 4]]) for k in (0, 4))
+        out += [jnp.concatenate([a, c], axis=1) for a, c in zip(low, high)]
+    return out
 
 
 def to_volume(d, wy, mz):
@@ -96,7 +112,8 @@
 
 def from_volume(v, wyt, mzt):
     e = mm(v.astype(BF), mzt).astype(BF)
-    return mm(wyt, jnp.concatenate([e[:, :256], e[:, 256:]], axis=0)).astype(BF)
+    half = e.shape[1] // 2
+    return mm(wyt, jnp.concatenate([e[:, :half], e[:, half:]], axis=0)).astype(BF)
 
 
 def shifted(v, u):
@@ -117,22 +134,35 @@
 
 
 def band_sums(g):
-    zp = lax.broadcasted_iota(jnp.int32, (16, 256), 1) // 8
-    acc = [jnp.zeros((16, 256), F32) for _ in range(3)]
+    cell = lax.broadcasted_iota(jnp.int32, (16, 128), 1) // 8
+    kept = [[jnp.zeros((16, 128), F32) for _ in range(3)] for _ in range(2)]
     for z in range(32):
-        t = zp - z
-        acc[z % 3] = jnp.where((t >= -1) & (t <= 1), g[z * 16:(z + 1) * 16], acc[z % 3])
+        for half in range(2):
+            if 16 * half - 1 <= z <= 16 * half + 16:
+                t = cell + (16 * half - z)
+                kept[half][z % 3] = jnp.where(t * t <= 1, g[z * 16:(z + 1) * 16, 128 * half:128 * (half + 1)], kept[half][z % 3])
     out = []
     for u in (-1, 0, 1):
-        z = zp - u
-        r = (z + 3) % 3
-        s = jnp.where(r == 0, acc[0], jnp.where(r == 1, acc[1], acc[2]))
-        s = jnp.where((z >= 0) & (z < 32), s, 0.0)
-        s = s[:, :128] + s[:, 128:]
-        for step in (64, 32, 16, 8):
-            s = s + roll(s, step, 1)
-        out.append(s)
+        total = None
+        for half in range(2):
+            z = cell + (16 * half - u)
+            r = (z + 3) % 3
+            s = jnp.where(r == 0, kept[half][0], jnp.where(r == 1, kept[half][1], kept[half][2]))
+            s = jnp.where((z >= 0) & (z < 32), s, 0.0)
+            total = s if total is None else total + s
+        out.append(total)
     return out
+
+
+def lane_sums(v):
+    same = (lax.broadcasted_iota(jnp.int32, (128, 128), 0) % 8 == lax.broadcasted_iota(jnp.int32, (128, 128), 1) % 8).astype(BF)
+    total = None
+    for _ in range(3):
+        part = v.astype(BF)
+        v = v - part.astype(F32)
+        term = mm(part, same)
+        total = term if total is None else total + term
+    return total
 
 
 def gates(hidden, back_active):
@@ -143,7 +173,7 @@
 def kernel(kspace_hbm, cotangent_hbm, mask, weight_in, weight_out, consistency, first_hbm, wide_hbm, rest_hbm,
            out, grad_in, grad_out,
            kspace, cotangent, first, wide, rest, wt, seml,
-           a1, r1, s2, r2, planes, band, zt, bh, send_p, recv_p, s3, r3, s4, r4, gr, ga, gs, gb, gt, gc,
+           a1, r1, s2, r2, planes, band, turned_band, zt, bh, send_p, recv_p, s3, r3, s4, r4, g_lanes, gr, ga, gs, gb, gt, gc,
            sem1, sem2, semh, semp, sem3, sem4, semg1, semg2, semg3):
     g = lax.axis_index("gy")
     j = lax.axis_index("gz")
@@ -151,16 +181,16 @@
     m = h * 8 + j
 
     def dev1(p):
-        return ((p // 8) * 16 + b, p % 8)
+        return (lax.div(p, 8) * 16 + b, lax.rem(p, 8))
 
     def dev2(p):
         return (h * 16 + p, j)
 
     def at_x(p):
-        mm_, bb = p % 16, p // 16
-        return ((mm_ // 8) * 16 + bb, mm_ % 8)
-
-    x = b * 16 + m
+        member, place = member_of(p)
+        return ((member // 8) * 16 + place, member % 8)
+
+    x = plane_of(m, b)
     right = at_x((x + 1) % 256)
     left = at_x((x + 255) % 256)
 
@@ -189,24 +219,21 @@
             src_ref=src, dst_ref=dst, send_sem=sems.at[0, i], recv_sem=sems.at[1, i],
             device_id=device, device_id_type=pl.DeviceIdType.MESH)
 
-    def send_all(me, dev, src, dst, sems):
-        def step(d, carry):
-            p = (me + d) % 16
-            remote(src(p), dst(me), sems, d, dev(p)).start()
-            return carry
-        lax.fori_loop(1, 16, step, 0)
-
-    def wait_all(me, dev, src, dst, sems):
-        def step(d, carry):
-            p = (me + d) % 16
-            q = (me + 16 - d) % 16
-            remote(src(p), dst(q), sems, d, dev(p)).wait_recv()
-            remote(src(p), dst(q), sems, d, dev(p)).wait_send()
-            return carry
-        lax.fori_loop(1, 16, step, 0)
-
-    ex1 = [(m, dev1, lambda p, f=f: a1.at[f, p], lambda p, f=f: r1.at[f, p], sem1.at[f]) for f in range(2)]
-    ex2 = [(b, dev2, lambda p, f=f: s2.at[f, p], lambda p, f=f: r2.at[f, p], sem2.at[f]) for f in range(2)]
+    def send_all(me, dev, src, dst, some, sems):
+        for d in range(1, 16):
+            p = lax.rem(me + d, 16)
+            remote(src(p), dst(me), sems, 0, dev(p)).start()
+
+    def wait_all(me, dev, src, dst, some, sems):
+        remote(*some, sems, 0, dev(lax.rem(me + 1, 16))).wait_recv()
+
+    def wait_sent(me, dev, src, dst, some, sems):
+        remote(*some, sems, 0, dev(lax.rem(me + 1, 16))).wait_send()
+
+    ex1 = [(m, dev1, lambda p, f=f: a1.at[f, p], lambda p, f=f: r1.at[f, p],
+            (a1.at[f, 0:15], r1.at[f, 0:15]), sem1.at[f]) for f in range(2)]
+    ex2 = [(b, dev2, lambda p, f=f: s2.at[f, p], lambda p, f=f: r2.at[f, p],
+            (s2.at[f, 0:15], r2.at[f, 0:15]), sem2.at[f]) for f in range(2)]
     loads[0].wait()
     for f, field in enumerate((kspace, cotangent)):
         loads[1 + f].wait()
@@ -246,6 +273,18 @@
 
     lax.fori_loop(0, 18, build, 0)
 
+    def turn(t, carry):
+        rows_at = pl.multiple_of(t * 256, 256)
+        turned_at = pl.multiple_of(t // 3 * 512, 512)
+        turned_band[t % 3, pl.ds(turned_at, 512), :] = band[pl.ds(rows_at, 256), :].T
+        return carry
+
+    lax.fori_loop(0, 9, turn, 0)
+
+    def halo_copies(f):
+        return (remote(planes.at[f, 1], planes.at[f, 0], semh, f, right),
+                remote(planes.at[f, 1], planes.at[f, 2], semh, 2 + f, left))
+
     for f in range(2):
         wait_all(*ex1[f])
         parts = [jnp.concatenate([r1[f, k], r1[f, 8 + k]], axis=0).astype(F32) for k in range(8)]
@@ -254,12 +293,10 @@
         send_all(*ex2[f])
         r2[f, b] = s2[f, b]
 
-    def halo_copies(f):
-        return (remote(planes.at[f, 1], planes.at[f, 0], semh, f, right),
-                remote(planes.at[f, 1], planes.at[f, 2], semh, 2 + f, left))
-
     loads[3].wait()
     loads[4].wait()
+    for f in range(2):
+        wait_sent(*ex1[f])
     for f in range(2):
         wait_all(*ex2[f])
         v = to_volume(r2[f].reshape(256, 256), (wy[...], wy_low[...]), (mz[...], mz_low[...]))
@@ -267,8 +304,8 @@
         for c in halo_copies(f):
             c.start()
 
-    has_left = jnp.where(x > 0, 1.0, 0.0)
-    has_right = jnp.where(x < 255, 1.0, 0.0)
+    for f in range(2):
+        wait_sent(*ex2[f])
     convolved = []
     for f in range(2):
         for c in halo_copies(f):
@@ -292,23 +329,20 @@
 
     active, back_hidden = gates(*convolved)
     for uy in (-1, 0, 1):
-        bh[uy + 1] = shifted(back_hidden, -uy).astype(BF)
-
-    def share(ux):
-        total = None
-        for uy in (-1, 0, 1):
-            row = (uy + 1) * 768 + (ux + 1) * 256
-            v = mm_nt(bh[uy + 1], band[row:row + 256, :])
-            total = v if total is None else total + v
-        return total
-
-    share_copies = (remote(send_p.at[0], recv_p.at[0], semp, 0, right),
-                    remote(send_p.at[1], recv_p.at[1], semp, 1, left))
-    send_p[0] = share(1).astype(BF)
-    share_copies[0].start()
-    send_p[1] = share(-1).astype(BF)
-    share_copies[1].start()
-    own = share(0)
+        bh[:, (uy + 1) * 512:(uy + 2) * 512] = shifted(back_hidden, -uy).astype(BF)
+
+    def share(side):
+        return mm(bh[...], turned_band[side])
+
+    away = x % 2
+    near = 1 - away
+    share_copies = []
+    for i, side in enumerate((away, near)):
+        send_p[i] = share(2 * side).astype(BF)
+        c = remote(send_p.at[i], recv_p.at[i], semp, i, at_x((x + 255 + 2 * side) % 256))
+        c.start()
+        share_copies.append(c)
+    own = share(1)
 
     lane = lax.broadcasted_iota(jnp.int32, (512, 256), 1)
     for f, v in enumerate((back_hidden, active)):
@@ -316,32 +350,40 @@
         zt[f, 0] = jnp.where(lane == 255, 0.0, roll(v, 255, 1)).astype(BF)
         zt[f, 1] = v.astype(BF)
         zt[f, 2] = jnp.where(lane == 0, 0.0, roll(v, 1, 1)).astype(BF)
-    gr[...] = jnp.zeros_like(gr)
-    slot = lax.broadcasted_iota(jnp.int32, (16, 128), 1) // 8
     for t in range(18):
         gm = mm(zt[t // 9, t % 9 // 3], planes[t // 9, t % 3])
-        for u, s in enumerate(band_sums(gm)):
+        for u, v in enumerate(band_sums(gm)):
             k = t * 3 + u
-            tile = slice((k // 7) * 16, (k // 7) * 16 + 16)
-            gr[tile, :] = jnp.where(slot == k % 7, s, gr[tile, :])
-    exg1 = (m, dev1, lambda p: gr.at[pl.ds(pl.multiple_of(p * 8, 8), 8)], lambda p: ga.at[p], semg1)
+            g_lanes[k * 16:(k + 1) * 16, :] = v
+    sums = lane_sums(g_lanes[...])
+    slot = lax.broadcasted_iota(jnp.int32, (16, 128), 1) // 8
+    for tile in range(8):
+        v = jnp.zeros((16, 128), F32)
+        for at in range(7):
+            k = 7 * tile + at
+            if k < 54:
+                v = jnp.where(slot == at, sums[k * 16:(k + 1) * 16], v)
+        gr[2 * tile] = v[:8]
+        gr[2 * tile + 1] = v[8:]
+    exg1 = (m, dev1, lambda p: gr.at[p], lambda p: ga.at[p], (gr.at[0:15], ga.at[0:15]), semg1)
     send_all(*exg1)
-    ga[m] = gr[pl.ds(pl.multiple_of(m * 8, 8), 8), :]
+    ga[m] = gr[m]
 
     for c in share_copies:
         c.wait()
-    back_image = own + recv_p[0].astype(F32) * has_left + recv_p[1].astype(F32) * has_right
+    inside = jnp.where((x > 0) & (x < 255), 1.0, 0.0)
+    back_image = own + recv_p[0].astype(F32) * inside + recv_p[1].astype(F32)
 
     s3[...] = from_volume(back_image, wyt[...], mzt[...]).reshape(16, 16, 256)
-    ex3 = (b, dev2, lambda p: s3.at[p], lambda p: r3.at[p], sem3)
+    ex3 = (b, dev2, lambda p: s3.at[p], lambda p: r3.at[p], (s3.at[0:15], r3.at[0:15]), sem3)
     send_all(*ex3)
     r3[b] = s3[b]
 
     wait_all(*exg1)
-    gs[...] = jnp.sum(ga[...], axis=0)
-    exg2 = (b, dev2, lambda p: gs, lambda p: gb.at[p], semg2)
+    gs[...] = jnp.broadcast_to(jnp.sum(ga[...], axis=0, keepdims=True), (16, 8, 128))
+    exg2 = (b, dev2, lambda p: gs.at[p], lambda p: gb.at[p], (gs.at[0:15], gb.at[0:15]), semg2)
     send_all(*exg2)
-    gb[b] = gs[...]
+    gb[b] = gs[b]
 
     wait_all(*ex3)
     rows = mm(pb[...], r3[...].reshape(256, 256))
@@ -350,16 +392,18 @@
         v = parts[k].astype(BF)
         s4[k] = v[:16]
         s4[8 + k] = v[16:]
-    ex4 = (m, dev1, lambda p: s4.at[p], lambda p: r4.at[p], sem4)
+    ex4 = (m, dev1, lambda p: s4.at[p], lambda p: r4.at[p], (s4.at[0:15], r4.at[0:15]), sem4)
     send_all(*ex4)
     r4[m] = s4[m]
 
     wait_all(*exg2)
-    gt[...] = jnp.sum(gb[...], axis=0)
-    exg3 = (m, dev1, lambda p: gt, lambda p: gc.at[p], semg3)
+    gt[...] = jnp.broadcast_to(jnp.sum(gb[...], axis=0, keepdims=True), (16, 8, 128))
+    exg3 = (m, dev1, lambda p: gt.at[p], lambda p: gc.at[p], (gt.at[0:15], gc.at[0:15]), semg3)
     send_all(*exg3)
-    gc[m] = gt[...]
-
+    gc[m] = gt[m]
+
+    for e in (ex3, ex4, exg1, exg2, exg3):
+        wait_sent(*e)
     wait_all(*ex4)
     spectrum = unpack(r4[...].reshape(256, 256), qyt[...], pxt[...])
     factor = mask[...].astype(F32)
@@ -409,13 +453,12 @@
             scratch(768, 256), scratch(512, 512), scratch(2816, 256), scratch(432, 128, kind=F32),
             pltpu.SemaphoreType.DMA((5,)),
             scratch(2, 16, 16, 256), scratch(2, 16, 16, 256), scratch(2, 16, 16, 256), scratch(2, 16, 16, 256),
-            scratch(2, 3, 256, 256), scratch(4608, 512), scratch(2, 3, 512, 256), scratch(3, 256, 512),
+            scratch(2, 3, 256, 256), scratch(4608, 512), scratch(3, 1536, 256), scratch(2, 3, 512, 256), scratch(256, 1536),
             scratch(2, 256, 256), scratch(2, 256, 256),
             scratch(16, 16, 256), scratch(16, 16, 256),
             scratch(16, 16, 256), scratch(16, 16, 256),
-            scratch(128, 128, kind=F32), scratch(16, 8, 128, kind=F32), scratch(8, 128, kind=F32),
-            scratch(16, 8, 128, kind=F32), scratch(8, 128, kind=F32), scratch(16, 8, 128, kind=F32),
-            pltpu.SemaphoreType.DMA((2, 2, 16)), pltpu.SemaphoreType.DMA((2, 2, 16)), sems(4), sems(2), sems(16), sems(16), sems(16), sems(16), sems(16),
+            scratch(864, 128, kind=F32), *[scratch(16, 8, 128, kind=F32) for _ in range(6)],
+            pltpu.SemaphoreType.DMA((2, 2, 1)), pltpu.SemaphoreType.DMA((2, 2, 1)), sems(4), sems(2), sems(1), sems(1), sems(1), sems(1), sems(1),
         ],
         compiler_params=pltpu.CompilerParams(
             collective_id=0, has_side_effects=True, vmem_limit_bytes=62 * 1024 * 1024),

time: 57.5 us -> 55.2 us (0.960)
  Pallas kernels: 52.7 us -> 50.4 us
    pallas_call x1, Pallas kernels: 52.7 us -> 50.4 us  [local(): pl.pallas_call(kernel, out_shape=(jax.ShapeDtypeStruct((64, 4, 256), F32)...]
where the time goes in v3:
time: 55.2 us; the launch traced here: 55 us
  Pallas kernels  50.4 us (91%)
  local copies, waits for them, and re-layouts  1.67 us (3%)
  other arithmetic  1.65 us (3%)
  between operations  1.29 us (2%)
    pallas_call x1, Pallas kernels, local(): pl.pallas_call(kernel, out_shape=(jax.ShapeDtypeStruct((64, 4, 256), F32)...  50.4 us
    unnamed x1, local copies, waits for them, and re-layouts  1.67 us
    mul x1, other arithmetic, local(): grad_out * scale  1.65 us

profile of v3, /device:TPU:1, one launch (start us, length us, event | category | flops | bytes accessed | tf_op | source)
XLA Modules:
  0.0 55.0 jit_solution(5592828102753609985)
XLA Ops:
  1.3 50.4 %cascade.1 = (f32[64,4,256]{2,1,0:T(4,128)}, f32[27,8,16]{2,1,0:T(8,128)}, f32[27,8,16]{2,1,0:T(8,128)}) custom-call(f32[64,4,256]{2,1,0:T(4,128)} %bitcast.17, f32[64,4,256]{2,1,0:T(4,128)} %bitcast.18, s32[4,8]{1,0:T(4,128)} %bitcast.23, bf16[27,8,16]{2,1,0:T(8,128)(2,1)} %bitcast.21, bf16[27,8,16]{2,1,0:T(8,128)(2,1)} %bitcast.22, ...), custom_call_target="tpu_custom_call" | custom-call | tf_op jit(solution)/shard_map/cascade/pallas_call | solution.py:446
  51.7 1.7 %broadcast_multiply_fusion = (f32[27,8,16]{2,1,0:T(8,128)}, f32[27,8,16]{2,1,0:T(8,128)}) fusion(f32[27,8,16]{2,1,0:T(8,128)} %get-tuple-element.8, f32[27,8,16]{2,1,0:T(8,128)} %get-tuple-element.7), kind=kLoop, calls=%fused_computation | loop fusion | flops 6912 | bytes 55296 | tf_op jit(solution)/shard_map/mul | solution.py:469
  53.3 1.7 %copy.14 = f32[2,4,8,4,256]{4,3,2,1,0:T(4,128)} copy(f32[2,4,8,4,256]{4,3,2,1,0:T(4,128)} %bitcast.16) | data formatting | bytes 524288

commit v4 on v3

--- a/solution.py
+++ b/solution.py
@@ -445,7 +445,7 @@
     grad_shape = jax.ShapeDtypeStruct((27, 8, 16), F32)
     out, grad_in, grad_out = pl.pallas_call(
         kernel,
-        out_shape=(jax.ShapeDtypeStruct((64, 4, 256), F32), grad_shape, grad_shape),
+        out_shape=(pltpu.VMEM((64, 4, 256), F32), pltpu.VMEM((27, 8, 16), F32), pltpu.VMEM((27, 8, 16), F32)),
         in_specs=[hbm, hbm, vmem, vmem, vmem, pl.BlockSpec(memory_space=pltpu.SMEM), hbm, hbm, hbm],
         out_specs=(vmem, vmem, vmem),
         scratch_shapes=[
@@ -461,7 +461,7 @@
             pltpu.SemaphoreType.DMA((2, 2, 1)), pltpu.SemaphoreType.DMA((2, 2, 1)), sems(4), sems(2), sems(1), sems(1), sems(1), sems(1), sems(1),
         ],
         compiler_params=pltpu.CompilerParams(
-            collective_id=0, has_side_effects=True, vmem_limit_bytes=62 * 1024 * 1024),
+            collective_id=0, has_side_effects=True, vmem_limit_bytes=60 * 1024 * 1024),
         name="cascade",
     )(kspace.reshape(64, 4, 256), cotangent.reshape(64, 4, 256), sampling_mask.T, w_in, w_out, consistency_weight, *map(jnp.asarray, tables()))
     scale = 1.0 / math.sqrt(2097152)

time: 55.2 us -> 52.6 us (0.953)
  local copies, waits for them, and re-layouts: 1.67 us -> 0.71 us
  other arithmetic: 1.65 us -> 0.7 us
  Pallas kernels: 50.4 us -> 49.7 us
    unnamed x1, local copies, waits for them, and re-layouts: 1.67 us -> 0.71 us
    mul x1, other arithmetic: 1.65 us -> 0.7 us  [local(): grad_out * scale]
    pallas_call x1, Pallas kernels: 50.4 us -> 49.7 us  [local(): pl.pallas_call(kernel, out_shape=(pltpu.VMEM((64, 4, 256), F32), pltpu.VM...]
where the time goes in v4:
time: 52.6 us; the launch traced here: 52.4 us
  Pallas kernels  49.7 us (94%)
  between operations  1.29 us (2%)
  local copies, waits for them, and re-layouts  0.71 us (1%)
  other arithmetic  0.7 us (1%)
    pallas_call x1, Pallas kernels, local(): pl.pallas_call(kernel, out_shape=(pltpu.VMEM((64, 4, 256), F32), pltpu.VM...  49.7 us

profile of v4, /device:TPU:1, one launch (start us, length us, event | category | flops | bytes accessed | tf_op | source)
XLA Modules:
  0.0 52.4 jit_solution(8873506175535563095)
XLA Ops:
  1.3 49.7 %cascade.1 = (f32[64,4,256]{2,1,0:T(4,128)S(1)}, f32[27,8,16]{2,1,0:T(8,128)S(1)}, f32[27,8,16]{2,1,0:T(8,128)S(1)}) custom-call(f32[64,4,256]{2,1,0:T(4,128)} %bitcast.17, f32[64,4,256]{2,1,0:T(4,128)} %bitcast.18, s32[4,8]{1,0:T(4,128)} %bitcast.23, bf16[27,8,16]{2,1,0:T(8,128)(2,1)} %bitcast.21, bf16[27,8,16]{2,1,0:T(8,128)(2,1)} %bitcast.22, ...), custom_call_target="tpu_custom_call" | custom-call | tf_op jit(solution)/shard_map/cascade/pallas_call | solution.py:446
  51.0 0.7 %copy.13 = f32[2,4,8,4,256]{4,3,2,1,0:T(4,128)} copy(f32[2,4,8,4,256]{4,3,2,1,0:T(4,128)S(1)} %bitcast.16) | data formatting | bytes 524288
  51.7 0.7 %broadcast_multiply_fusion = (f32[27,8,16]{2,1,0:T(8,128)}, f32[27,8,16]{2,1,0:T(8,128)}) fusion(f32[27,8,16]{2,1,0:T(8,128)S(1)} %get-tuple-element.8, f32[27,8,16]{2,1,0:T(8,128)S(1)} %get-tuple-element.7), kind=kLoop, calls=%fused_computation | loop fusion | flops 6912 | bytes 55296 | tf_op jit(solution)/shard_map/mul | solution.py:469

commit v5 on v4

--- a/solution.py
+++ b/solution.py
@@ -103,11 +103,11 @@
 
 
 def to_volume(d, wy, mz):
-    cs = mm(wy[0], d) + mm(wy[1], d)
+    cs = mm(jnp.concatenate(wy, axis=1), jnp.concatenate([d, d], axis=0))
     cs = jnp.concatenate([cs[:256], cs[256:]], axis=1)
     high = cs.astype(BF)
     low = (cs - high.astype(F32)).astype(BF)
-    return mm(high, mz[0]) + (mm(high, mz[1]) + mm(low, mz[0]))
+    return mm(jnp.concatenate([high, high, low], axis=1), jnp.concatenate([mz[0], mz[1], mz[0]], axis=0))
 
 
 def from_volume(v, wyt, mzt):
@@ -194,21 +194,18 @@
     right = at_x((x + 1) % 256)
     left = at_x((x + 255) % 256)
 
-    barrier = pltpu.get_barrier_semaphore()
-
-    def greet(d, carry):
-        pl.semaphore_signal(barrier, inc=1, device_id=dev1((m + d) % 16), device_id_type=pl.DeviceIdType.MESH)
-        pl.semaphore_signal(barrier, inc=1, device_id=dev2((b + d) % 16), device_id_type=pl.DeviceIdType.MESH)
-        return carry
-
-    lax.fori_loop(1, 16, greet, 0)
-    pl.semaphore_signal(barrier, inc=1, device_id=right, device_id_type=pl.DeviceIdType.MESH)
-    pl.semaphore_signal(barrier, inc=1, device_id=left, device_id_type=pl.DeviceIdType.MESH)
-
     loads = [pltpu.make_async_copy(src, dst, seml.at[i]) for i, (src, dst) in enumerate((
         (first_hbm, first), (kspace_hbm, kspace), (cotangent_hbm, cotangent), (rest_hbm, rest), (wide_hbm, wide)))]
     for c in loads:
         c.start()
+    barrier = pltpu.get_barrier_semaphore()
+
+    for d in range(1, 16):
+        pl.semaphore_signal(barrier, inc=1, device_id=dev1(lax.rem(m + d, 16)), device_id_type=pl.DeviceIdType.MESH)
+        pl.semaphore_signal(barrier, inc=1, device_id=dev2(lax.rem(b + d, 16)), device_id_type=pl.DeviceIdType.MESH)
+    pl.semaphore_signal(barrier, inc=1, device_id=right, device_id_type=pl.DeviceIdType.MESH)
+    pl.semaphore_signal(barrier, inc=1, device_id=left, device_id_type=pl.DeviceIdType.MESH)
+
     qy, px, pbt = (first.at[256 * i:256 * (i + 1)] for i in range(3))
     wyt, mzt = (wide.at[256 * i:256 * (i + 1)] for i in range(2))
     wy, wy_low, mz, mz_low = (rest.at[512 * i:512 * (i + 1)] for i in range(4))
@@ -220,7 +217,7 @@
             device_id=device, device_id_type=pl.DeviceIdType.MESH)
 
     def send_all(me, dev, src, dst, some, sems):
-        for d in range(1, 16):
+        for d in (8, 7, 9, 6, 10, 5, 11, 4, 12, 3, 13, 2, 14, 1, 15):
             p = lax.rem(me + d, 16)
             remote(src(p), dst(me), sems, 0, dev(p)).start()
 

time: 52.6 us -> 51.5 us (0.979)
  Pallas kernels: 49.7 us -> 48.7 us
    pallas_call x1, Pallas kernels: 49.7 us -> 48.7 us  [local(): pl.pallas_call(kernel, out_shape=(pltpu.VMEM((64, 4, 256), F32), pltpu.VM...]
where the time goes in v5:
time: 51.5 us; the launch traced here: 51.4 us
  Pallas kernels  48.7 us (95%)
  between operations  1.29 us (3%)
  local copies, waits for them, and re-layouts  0.71 us (1%)
  other arithmetic  0.7 us (1%)
    pallas_call x1, Pallas kernels, local(): pl.pallas_call(kernel, out_shape=(pltpu.VMEM((64, 4, 256), F32), pltpu.VM...  48.7 us

profile of v5, /device:TPU:1, one launch (start us, length us, event | category | flops | bytes accessed | tf_op | source)
XLA Modules:
  0.0 51.4 jit_solution(14200430108276900970)
XLA Ops:
  1.3 48.7 %cascade.1 = (f32[64,4,256]{2,1,0:T(4,128)S(1)}, f32[27,8,16]{2,1,0:T(8,128)S(1)}, f32[27,8,16]{2,1,0:T(8,128)S(1)}) custom-call(f32[64,4,256]{2,1,0:T(4,128)} %bitcast.17, f32[64,4,256]{2,1,0:T(4,128)} %bitcast.18, s32[4,8]{1,0:T(4,128)} %bitcast.23, bf16[27,8,16]{2,1,0:T(8,128)(2,1)} %bitcast.21, bf16[27,8,16]{2,1,0:T(8,128)(2,1)} %bitcast.22, ...), custom_call_target="tpu_custom_call" | custom-call | tf_op jit(solution)/shard_map/cascade/pallas_call | solution.py:443
  50.0 0.7 %copy.13 = f32[2,4,8,4,256]{4,3,2,1,0:T(4,128)} copy(f32[2,4,8,4,256]{4,3,2,1,0:T(4,128)S(1)} %bitcast.16) | data formatting | bytes 524288
  50.7 0.7 %broadcast_multiply_fusion = (f32[27,8,16]{2,1,0:T(8,128)}, f32[27,8,16]{2,1,0:T(8,128)}) fusion(f32[27,8,16]{2,1,0:T(8,128)S(1)} %get-tuple-element.8, f32[27,8,16]{2,1,0:T(8,128)S(1)} %get-tuple-element.7), kind=kLoop, calls=%fused_computation | loop fusion | flops 6912 | bytes 55296 | tf_op jit(solution)/shard_map/mul | solution.py:466

commit v6 on v5

--- a/solution.py
+++ b/solution.py
@@ -399,7 +399,7 @@
     send_all(*exg3)
     gc[m] = gt[m]
 
-    for e in (ex3, ex4, exg1, exg2, exg3):
+    for e in (ex3, exg1, exg2):
         wait_sent(*e)
     wait_all(*ex4)
     spectrum = unpack(r4[...].reshape(256, 256), qyt[...], pxt[...])
@@ -411,6 +411,8 @@
         scaled = (rows.reshape(8, 8, 256) * sampled[None]).reshape(64, 256)
         out[:, z, :] = rows - scaled + spectrum[z * 64:(z + 1) * 64]
 
+    for e in (ex4, exg3):
+        wait_sent(*e)
     wait_all(*exg3)
     turned = gc[...].reshape(128, 128).T
     for t in range(8):

time: 51.5 us -> 51.5 us (level)
  no operation moved by 1% of the time
where the time goes in v6:
time: 51.5 us; the launch traced here: 51.4 us
  Pallas kernels  48.7 us (95%)
  between operations  1.29 us (3%)
  local copies, waits for them, and re-layouts  0.71 us (1%)
  other arithmetic  0.7 us (1%)
    pallas_call x1, Pallas kernels, local(): pl.pallas_call(kernel, out_shape=(pltpu.VMEM((64, 4, 256), F32), pltpu.VM...  48.7 us

profile of v6, /device:TPU:1, one launch (start us, length us, event | category | flops | bytes accessed | tf_op | source)
XLA Modules:
  0.0 51.4 jit_solution(13352753020623155731)
XLA Ops:
  1.3 48.7 %cascade.1 = (f32[64,4,256]{2,1,0:T(4,128)S(1)}, f32[27,8,16]{2,1,0:T(8,128)S(1)}, f32[27,8,16]{2,1,0:T(8,128)S(1)}) custom-call(f32[64,4,256]{2,1,0:T(4,128)} %bitcast.17, f32[64,4,256]{2,1,0:T(4,128)} %bitcast.18, s32[4,8]{1,0:T(4,128)} %bitcast.23, bf16[27,8,16]{2,1,0:T(8,128)(2,1)} %bitcast.21, bf16[27,8,16]{2,1,0:T(8,128)(2,1)} %bitcast.22, ...), custom_call_target="tpu_custom_call" | custom-call | tf_op jit(solution)/shard_map/cascade/pallas_call | solution.py:445
  50.0 0.7 %copy.13 = f32[2,4,8,4,256]{4,3,2,1,0:T(4,128)} copy(f32[2,4,8,4,256]{4,3,2,1,0:T(4,128)S(1)} %bitcast.16) | data formatting | bytes 524288
  50.7 0.7 %broadcast_multiply_fusion = (f32[27,8,16]{2,1,0:T(8,128)}, f32[27,8,16]{2,1,0:T(8,128)}) fusion(f32[27,8,16]{2,1,0:T(8,128)S(1)} %get-tuple-element.8, f32[27,8,16]{2,1,0:T(8,128)S(1)} %get-tuple-element.7), kind=kLoop, calls=%fused_computation | loop fusion | flops 6912 | bytes 55296 | tf_op jit(solution)/shard_map/mul | solution.py:468
